TPU v7x, 256 devices: a whole 4x4x8 slice. The times are simulated.
256 devices in a mesh: team: 64 (over z, y_lo, x), rep: 2 (over core), feat: 2 (over y_hi).
Axes of the slice: x: 4, y: 4 (y_hi: 2, y_lo: 2; y = y_hi * 2 + y_lo), z: 8, core: 2. Of those that a mesh axis runs over, the one named last changes fastest.
Arguments:
- node_feats: bfloat16 [262144, 128], P('team'), may hold values from -6 to 6
- tile_vals: bfloat16 [1024, 2, 5, 8, 128, 128], P('team', 'feat', None, 'rep'), may hold values from -0.125 to 0.125
- tile_cols: int32 [1024, 2, 5, 8], P('team', 'feat', None, 'rep'), may hold values from 0 to 31
- tile_count: int32 [1024, 2, 5], P('team', 'feat'), may hold values from 0 to 8
- node_count: int32 [64], P('team'), may hold values from 2048 to 4096
- weight: bfloat16 [128, 256], replicated, may hold values from -0.5 to 0.5
- bias: bfloat16 [256], replicated, may hold values from -3 to 3
Outputs:
- hidden: bfloat16 [262144, 256], P(('team', 'rep'), 'feat')
All inputs are finite; a program needn't handle non-finite values.
Results may differ from a plain program's by a relative error of at most 0.0044.
Values may be sent and summed in bfloat16 or wider, within the bound.
No kernel may reach another device: no remote copies, remote signals or barrier semaphores. Data moves between devices by JAX's collectives and lax.ppermute only.
A program may use at most 128 MiB of HBM per device.

v0:
```python
import jax
import jax.numpy as jnp
from jax import lax
from jax.sharding import PartitionSpec as P


def passed_along(value, axis, by):
    devices = lax.axis_size(axis)
    return lax.ppermute(value, axis, [(i, (i + by) % devices) for i in range(devices)])


def local(node_feats, tile_vals, tile_cols, tile_count, node_count, weight, bias):
    slab_rows, feat_width = node_feats.shape
    tile_size = tile_vals.shape[-1]
    span_count = tile_vals.shape[2]
    reach_count = span_count // 2
    slots_local = tile_vals.shape[3]
    groups_local = tile_vals.shape[0]
    row_pos = jnp.arange(slab_rows, dtype=jnp.int32)
    visible = jnp.where((row_pos < node_count[0])[:, None], node_feats, jnp.zeros_like(node_feats))
    tiles = tile_vals[:, 0]
    columns = tile_cols[:, 0]
    counts = tile_count[:, 0]
    slot_ids = lax.axis_index("rep") * slots_local + jnp.arange(slots_local, dtype=jnp.int32)

    def contribute(total, block, offset):
        panels = block.reshape(slab_rows // tile_size, tile_size, feat_width)
        tile_now = lax.dynamic_index_in_dim(tiles, offset, 1, keepdims=False)
        cols_now = lax.dynamic_index_in_dim(columns, offset, 1, keepdims=False)
        count_now = lax.dynamic_index_in_dim(counts, offset, 1, keepdims=False)
        live = slot_ids[None, :] < count_now[:, None]
        picked = jnp.where(live[:, :, None, None], panels[cols_now], jnp.zeros((), panels.dtype))
        return total + jnp.einsum(
            "gsij,gsjc->gic", tile_now, picked, preferred_element_type=jnp.float32
        )

    total = jnp.zeros((groups_local, tile_size, feat_width), jnp.float32)
    moving = passed_along(visible, "team", reach_count)
    total = contribute(total, moving, 0)

    def advance(step, carry):
        running, current = carry
        current = passed_along(current, "team", -1)
        return (contribute(running, current, step), current)

    total, moving = lax.fori_loop(1, span_count, advance, (total, moving))
    summed = lax.psum_scatter(total, "rep", scatter_dimension=0, tiled=True)
    own_agg = summed.astype(jnp.bfloat16)
    hid_width = weight.shape[1]
    feat_devices = lax.axis_size("feat")
    share = hid_width // feat_devices
    start_col = lax.axis_index("feat") * share
    weight_own = lax.dynamic_slice_in_dim(weight, start_col, share, 1)
    bias_own = lax.dynamic_slice_in_dim(bias, start_col, share, 0).astype(jnp.float32)
    product = jnp.einsum(
        "gkic,ch->gkih",
        lax.all_gather(own_agg[:, None], "feat", axis=1, tiled=True),
        weight_own,
        preferred_element_type=jnp.float32,
    )
    result = jnp.maximum(product + bias_own, 0.0)
    result = result.reshape(-1, share)
    rows_here = result.shape[0]
    out_pos = lax.axis_index("rep") * rows_here + jnp.arange(rows_here, dtype=jnp.int32)
    result = jnp.where((out_pos < node_count[0])[:, None], result, jnp.zeros_like(result))
    return result.astype(jnp.bfloat16)


def solution(mesh):
    return jax.shard_map(
        local,
        mesh=mesh,
        in_specs=(
            P("team", None),
            P("team", "feat", None, "rep", None, None),
            P("team", "feat", None, "rep"),
            P("team", "feat", None),
            P("team"),
            P(),
            P(),
        ),
        out_specs=P(("team", "rep"), "feat"),
        check_vma=False,
    )
```

profile of v0, /device:TPU:1, one launch (start us, length us, event | category | flops | bytes accessed | tf_op | source)
XLA Modules:
  0.0 208.0 jit_solution(9863797285955698772)
XLA Ops:
  7.2 3.4 %broadcast_select_fusion = bf16[4096,128]{1,0:T(8,128)(2,1)S(1)} fusion(bf16[4096,128]{1,0:T(8,128)(2,1)} %param.9, pred[4096]{0:T(1024)(128)(4,1)S(1)} %iota_compare_fusion), kind=kLoop, calls=%fused_computation.29 | loop fusion | flops 524288 | bytes 2101248 | tf_op jit(solution)/shard_map/jit(_where)/select_n | solution.py:20
  10.6 3.7 %collective-permute-start.1 = (bf16[4096,128]{1,0:T(8,128)(2,1)S(1)}, bf16[4096,128]{1,0:T(8,128)(2,1)S(1)}, u32[]{:S(2)}, u32[]{:S(2)}) collective-permute-start(bf16[4096,128]{1,0:T(8,128)(2,1)S(1)} %broadcast_select_fusion), channel_id=1, source_target_pairs={{0,8},{4,12},{8,16},{12,20},{16,24},{20,28},{24,32},{28,36},{32,40... | collective-permute-start | bytes 3145736 | tf_op jit(solution)/shard_map/ppermute | solution.py:9
  15.1 12.8 %copy.28 = bf16[16,1,5,4,128,128]{5,4,3,0,2,1:T(8,128)(2,1)} copy(bf16[16,1,5,4,128,128]{5,4,3,2,1,0:T(8,128)(2,1)} %param.10) | data formatting | bytes 20971520 | tf_op args[1]
  28.0 15.4 %collective-permute-done.1 = bf16[4096,128]{1,0:T(8,128)(2,1)S(1)} collective-permute-done((bf16[4096,128]{1,0:T(8,128)(2,1)S(1)}, bf16[4096,128]{1,0:T(8,128)(2,1)S(1)}, u32[]{:S(2)}, u32[]{:S(2)}) %collective-permute-start.1) | collective-permute-done | bytes 1048608 | tf_op jit(solution)/shard_map/ppermute | solution.py:9
  44.4 2.9 %copy.16 = bf16[64,128,128]{1,2,0:T(8,128)(2,1)} copy(bf16[64,128,128]{2,1,0:T(8,128)(2,1)S(1)} %gather_fusion.1) | data formatting | bytes 4194304 | tf_op jit(solution)/shard_map/gather | solution.py:32
  47.4 3.0 %fusion.24 = f32[16,128,128]{1,2,0:T(8,128)S(1)} fusion(bf16[16,1,5,4,128,128]{5,4,3,0,2,1:T(8,128)(2,1)} %copy.28, bf16[16,4,128,128]{2,3,1,0:T(8,128)(2,1)} %bitcast.76, pred[16,4]{1,0:T(8,128)(4,1)S(1)} %broadcast_compare_fusion.1), kind=kOutput, calls=%fused_computation.23 | convolution fusion | flops 269484032 | bytes 5242944 | tf_op jit(solution)/shard_map/gsij,gsjc->gic/dot_general | solution.py:33
  50.3 1.3 copy.19
  51.7 118.5 %while.18 = (s32[]{:T(128)}, f32[16,128,128]{2,1,0:T(8,128)}, bf16[4096,128]{1,0:T(8,128)(2,1)S(1)}, bf16[16,5,4,128,128]{4,3,2,0,1:T(8,128)(2,1)}, s32[16,5]{0,...) while((s32[]{:T(128)}, f32[16,128,128]{2,1,0:T(8,128)}, ...), condition=%wide.region_1.2_spmd.clone, body=%wide.region_0.1_spmd.clone.sunk | while | flops 269747456 | bytes 16783912 | solution.py:46
  51.7 2.4 %collective-permute-start = (bf16[4096,128]{1,0:T(8,128)(2,1)S(1)}, bf16[4096,128]{1,0:T(8,128)(2,1)S(1)}, u32[]{:S(2)}, u32[]{:S(2)}) collective-permute-start(bf16[4096,128]{1,0:T(8,128)(2,1)S(1)} %get-tuple-element.284), channel_id=1, source_target_pairs={{0,252},{4,0},{8,4},{12,8},{16,12},{20,16},{24,20},{28,24},{32,28}... | collective-permute-start | bytes 3145736 | tf_op jit(solution)/shard_map/while/body/eval_jaxpr/ppermute | solution.py:9
  55.0 20.0 %collective-permute-done = bf16[4096,128]{1,0:T(8,128)(2,1)S(1)} collective-permute-done((bf16[4096,128]{1,0:T(8,128)(2,1)S(1)}, bf16[4096,128]{1,0:T(8,128)(2,1)S(1)}, u32[]{:S(2)}, u32[]{:S(2)}) %collective-permute-start) | collective-permute-done | bytes 1048608 | tf_op jit(solution)/shard_map/while/body/eval_jaxpr/ppermute | solution.py:9
  76.0 3.6 %fusion.42 = f32[16,128,128]{2,1,0:T(8,128)} fusion(f32[16,128,128]{2,1,0:T(8,128)} %get-tuple-element.283, bf16[16,4,128,128]{3,2,1,0:T(8,128)(2,1)S(1)} %bitcast.72, pred[16,4]{1,0:T(8,128)(4,1)S(1)} %broadcast_compare_fusion.3, bf16[16,5,4,128,128]{4,3,2,0,1:T(8,128)(2,1)} %get-tuple-element.295, s32[]{:T(128)S(6)} %select_n.100), kind=kOutput, calls=%fused_computation.9.clone.1 | convolution fusion | flops 269746176 | bytes 6291524 | tf_op jit(solution)/shard_map/while/body/eval_jaxpr/gsij,gsjc->gic/dot_general | solution.py:33
  79.7 6.4 %collective-permute-start = (bf16[4096,128]{1,0:T(8,128)(2,1)S(1)}, bf16[4096,128]{1,0:T(8,128)(2,1)S(1)}, u32[]{:S(2)}, u32[]{:S(2)}) collective-permute-start(bf16[4096,128]{1,0:T(8,128)(2,1)S(1)} %get-tuple-element.284), channel_id=1, source_target_pairs={{0,252},{4,0},{8,4},{12,8},{16,12},{20,16},{24,20},{28,24},{32,28}... | collective-permute-start | bytes 3145736 | tf_op jit(solution)/shard_map/while/body/eval_jaxpr/ppermute | solution.py:9
  87.1 19.0 %collective-permute-done = bf16[4096,128]{1,0:T(8,128)(2,1)S(1)} collective-permute-done((bf16[4096,128]{1,0:T(8,128)(2,1)S(1)}, bf16[4096,128]{1,0:T(8,128)(2,1)S(1)}, u32[]{:S(2)}, u32[]{:S(2)}) %collective-permute-start) | collective-permute-done | bytes 1048608 | tf_op jit(solution)/shard_map/while/body/eval_jaxpr/ppermute | solution.py:9
  107.0 3.6 %fusion.42 = f32[16,128,128]{2,1,0:T(8,128)} fusion(f32[16,128,128]{2,1,0:T(8,128)} %get-tuple-element.283, bf16[16,4,128,128]{3,2,1,0:T(8,128)(2,1)S(1)} %bitcast.72, pred[16,4]{1,0:T(8,128)(4,1)S(1)} %broadcast_compare_fusion.3, bf16[16,5,4,128,128]{4,3,2,0,1:T(8,128)(2,1)} %get-tuple-element.295, s32[]{:T(128)S(6)} %select_n.100), kind=kOutput, calls=%fused_computation.9.clone.1 | convolution fusion | flops 269746176 | bytes 6291524 | tf_op jit(solution)/shard_map/while/body/eval_jaxpr/gsij,gsjc->gic/dot_general | solution.py:33
  110.7 6.5 %collective-permute-start = (bf16[4096,128]{1,0:T(8,128)(2,1)S(1)}, bf16[4096,128]{1,0:T(8,128)(2,1)S(1)}, u32[]{:S(2)}, u32[]{:S(2)}) collective-permute-start(bf16[4096,128]{1,0:T(8,128)(2,1)S(1)} %get-tuple-element.284), channel_id=1, source_target_pairs={{0,252},{4,0},{8,4},{12,8},{16,12},{20,16},{24,20},{28,24},{32,28}... | collective-permute-start | bytes 3145736 | tf_op jit(solution)/shard_map/while/body/eval_jaxpr/ppermute | solution.py:9
  118.2 18.1 %collective-permute-done = bf16[4096,128]{1,0:T(8,128)(2,1)S(1)} collective-permute-done((bf16[4096,128]{1,0:T(8,128)(2,1)S(1)}, bf16[4096,128]{1,0:T(8,128)(2,1)S(1)}, u32[]{:S(2)}, u32[]{:S(2)}) %collective-permute-start) | collective-permute-done | bytes 1048608 | tf_op jit(solution)/shard_map/while/body/eval_jaxpr/ppermute | solution.py:9
  137.2 3.6 %fusion.42 = f32[16,128,128]{2,1,0:T(8,128)} fusion(f32[16,128,128]{2,1,0:T(8,128)} %get-tuple-element.283, bf16[16,4,128,128]{3,2,1,0:T(8,128)(2,1)S(1)} %bitcast.72, pred[16,4]{1,0:T(8,128)(4,1)S(1)} %broadcast_compare_fusion.3, bf16[16,5,4,128,128]{4,3,2,0,1:T(8,128)(2,1)} %get-tuple-element.295, s32[]{:T(128)S(6)} %select_n.100), kind=kOutput, calls=%fused_computation.9.clone.1 | convolution fusion | flops 269746176 | bytes 6291524 | tf_op jit(solution)/shard_map/while/body/eval_jaxpr/gsij,gsjc->gic/dot_general | solution.py:33
  140.9 6.5 %collective-permute-start = (bf16[4096,128]{1,0:T(8,128)(2,1)S(1)}, bf16[4096,128]{1,0:T(8,128)(2,1)S(1)}, u32[]{:S(2)}, u32[]{:S(2)}) collective-permute-start(bf16[4096,128]{1,0:T(8,128)(2,1)S(1)} %get-tuple-element.284), channel_id=1, source_target_pairs={{0,252},{4,0},{8,4},{12,8},{16,12},{20,16},{24,20},{28,24},{32,28}... | collective-permute-start | bytes 3145736 | tf_op jit(solution)/shard_map/while/body/eval_jaxpr/ppermute | solution.py:9
  148.4 17.1 %collective-permute-done = bf16[4096,128]{1,0:T(8,128)(2,1)S(1)} collective-permute-done((bf16[4096,128]{1,0:T(8,128)(2,1)S(1)}, bf16[4096,128]{1,0:T(8,128)(2,1)S(1)}, u32[]{:S(2)}, u32[]{:S(2)}) %collective-permute-start) | collective-permute-done | bytes 1048608 | tf_op jit(solution)/shard_map/while/body/eval_jaxpr/ppermute | solution.py:9
  166.5 3.6 %fusion.42 = f32[16,128,128]{2,1,0:T(8,128)} fusion(f32[16,128,128]{2,1,0:T(8,128)} %get-tuple-element.283, bf16[16,4,128,128]{3,2,1,0:T(8,128)(2,1)S(1)} %bitcast.72, pred[16,4]{1,0:T(8,128)(4,1)S(1)} %broadcast_compare_fusion.3, bf16[16,5,4,128,128]{4,3,2,0,1:T(8,128)(2,1)} %get-tuple-element.295, s32[]{:T(128)S(6)} %select_n.100), kind=kOutput, calls=%fused_computation.9.clone.1 | convolution fusion | flops 269746176 | bytes 6291524 | tf_op jit(solution)/shard_map/while/body/eval_jaxpr/gsij,gsjc->gic/dot_general | solution.py:33
  170.3 18.1 %reduce-scatter.2.cloned.1.call-done = f32[8,128,128]{2,1,0:T(8,128)} async-done(((f32[16,128,128]{2,1,0:T(8,128)}), f32[8,128,128]{2,1,0:T(8,128)}) %reduce-scatter.2.cloned.1.call-update) | async-done | bytes 524304 | tf_op jit(solution)/shard_map/reduce_scatter | solution.py:47
  188.4 1.1 convert_element_type.9
  189.5 10.3 %all-gather = bf16[8,256,128]{2,1,0:T(8,128)(2,1)S(1)} all-gather(bf16[8,128,128]{2,1,0:T(8,128)(2,1)S(1)} %convert_element_type.9), channel_id=2, replica_groups=mesh['team'=64,'rep'=2,'feat'=2] {'feat'}, dimensions={1}, use_global_device_ids=true | all-gather | bytes 786432 | tf_op jit(solution)/shard_map/all_gather | solution.py:57
  200.1 1.1 fusion.28
  (57 shorter events, 10.2 us)
Async XLA Ops:
  6.5 193.2 %copy-start = (bf16[128,256]{1,0:T(8,128)(2,1)S(1)}, bf16[128,256]{1,0:T(8,128)(2,1)}, u32[]{:S(2)}) copy-start(bf16[128,256]{1,0:T(8,128)(2,1)} %param.14) | copy-start | bytes 196612
  6.5 181.8 %reduce-scatter.2.cloned.1.call-start = ((), (), s32[]{:S(2)}) async-start(), calls=%async_computation.1 | async-start | bytes 1572864 | tf_op jit(solution)/shard_map/reduce_scatter | solution.py:47
  10.6 32.8 %collective-permute-start.1 = (bf16[4096,128]{1,0:T(8,128)(2,1)S(1)}, bf16[4096,128]{1,0:T(8,128)(2,1)S(1)}, u32[]{:S(2)}, u32[]{:S(2)}) collective-permute-start(bf16[4096,128]{1,0:T(8,128)(2,1)S(1)} %broadcast_select_fusion), channel_id=1, source_target_pairs={{0,8},{4,12},{8,16},{12,20},{16,24},{20,28},{24,32},{28,36},{32,40... | collective-permute-start | bytes 3145736 | tf_op jit(solution)/shard_map/ppermute | solution.py:9
  15.1 12.8 %copy-start.1 = (s32[16,1,5]{0,1,2:T(1,128)S(1)}, s32[16,1,5]{0,1,2:T(1,128)}, u32[]{:S(2)}) copy-start(s32[16,1,5]{0,1,2:T(1,128)} %param.12) | copy-start | bytes 964
  51.6 118.6 %copy-start.2 = (bf16[256]{0:T(256)(128)(2,1)S(1)}, bf16[256]{0:T(256)(128)(2,1)}, u32[]{:S(2)}) copy-start(bf16[256]{0:T(256)(128)(2,1)} %param.15) | copy-start | bytes 1540
  51.7 23.4 %collective-permute-start = (bf16[4096,128]{1,0:T(8,128)(2,1)S(1)}, bf16[4096,128]{1,0:T(8,128)(2,1)S(1)}, u32[]{:S(2)}, u32[]{:S(2)}) collective-permute-start(bf16[4096,128]{1,0:T(8,128)(2,1)S(1)} %get-tuple-element.284), channel_id=1, source_target_pairs={{0,252},{4,0},{8,4},{12,8},{16,12},{20,16},{24,20},{28,24},{32,28}... | collective-permute-start | bytes 3145736 | tf_op jit(solution)/shard_map/while/body/eval_jaxpr/ppermute | solution.py:9
  79.7 26.3 %collective-permute-start = (bf16[4096,128]{1,0:T(8,128)(2,1)S(1)}, bf16[4096,128]{1,0:T(8,128)(2,1)S(1)}, u32[]{:S(2)}, u32[]{:S(2)}) collective-permute-start(bf16[4096,128]{1,0:T(8,128)(2,1)S(1)} %get-tuple-element.284), channel_id=1, source_target_pairs={{0,252},{4,0},{8,4},{12,8},{16,12},{20,16},{24,20},{28,24},{32,28}... | collective-permute-start | bytes 3145736 | tf_op jit(solution)/shard_map/while/body/eval_jaxpr/ppermute | solution.py:9
  110.7 25.5 %collective-permute-start = (bf16[4096,128]{1,0:T(8,128)(2,1)S(1)}, bf16[4096,128]{1,0:T(8,128)(2,1)S(1)}, u32[]{:S(2)}, u32[]{:S(2)}) collective-permute-start(bf16[4096,128]{1,0:T(8,128)(2,1)S(1)} %get-tuple-element.284), channel_id=1, source_target_pairs={{0,252},{4,0},{8,4},{12,8},{16,12},{20,16},{24,20},{28,24},{32,28}... | collective-permute-start | bytes 3145736 | tf_op jit(solution)/shard_map/while/body/eval_jaxpr/ppermute | solution.py:9
  140.9 24.6 %collective-permute-start = (bf16[4096,128]{1,0:T(8,128)(2,1)S(1)}, bf16[4096,128]{1,0:T(8,128)(2,1)S(1)}, u32[]{:S(2)}, u32[]{:S(2)}) collective-permute-start(bf16[4096,128]{1,0:T(8,128)(2,1)S(1)} %get-tuple-element.284), channel_id=1, source_target_pairs={{0,252},{4,0},{8,4},{12,8},{16,12},{20,16},{24,20},{28,24},{32,28}... | collective-permute-start | bytes 3145736 | tf_op jit(solution)/shard_map/while/body/eval_jaxpr/ppermute | solution.py:9
Sparse Core Ops, SparseCore 0:
  170.3 18.0 reduce-scatter.1
where the time goes:
time: 208 us
  waiting for transfers between devices  108 us (52%)
  starting transfers between devices  25.4 us (12%)
  local copies, waits for them, and re-layouts  23 us (11%)
  matrix products  17.7 us (9%)
  between operations  14.2 us (7%)
  blocking collectives  10.3 us (5%)
  other arithmetic  9.53 us (5%)
    ppermute x5, waiting for transfers between devices, passed_along(): lax.ppermute(value, axis, [(i, (i + by) % devices) for i in range(devices)])  89.7 us
    ppermute x5, starting transfers between devices, passed_along(): lax.ppermute(value, axis, [(i, (i + by) % devices) for i in range(devices)])  25.4 us
    reduce_scatter x1, waiting for transfers between devices, local(): summed = lax.psum_scatter(total, 'rep', scatter_dimension=0, tiled=True)  18.1 us
    dot_general x5, matrix products, contribute(): jnp.einsum('gsij,gsjc->gic', tile_now, picked, preferred_element_type=jnp...  17.4 us
    unnamed x9, local copies, waits for them, and re-layouts  14.1 us
    all_gather x1, blocking collectives, local(): lax.all_gather(own_agg[:, None], 'feat', axis=1, tiled=True)  10.3 us
    gather x6, local copies, waits for them, and re-layouts, contribute(): panels[cols_now]  7.68 us
  transfers between devices with their start and end apart: 6, of which 6 were waited for; matrix products, arithmetic and copies ran while one was open for 8% of the time, Pallas kernels for 0%

commit v1 on v0

v1 whole, which is shorter than its diff:
```python
import functools

import jax
import jax.numpy as jnp
from jax import lax
from jax.experimental import pallas as pl
from jax.experimental.pallas import tpu as pltpu
from jax.sharding import PartitionSpec as P

AXES = ("team", "rep", "feat")
VMEM_LIMIT = 24 * 1024 * 1024


def permutation(move):
    teams, reps, feats = (lax.axis_size(a) for a in AXES)
    pairs = []
    for t in range(teams):
        for r in range(reps):
            for f in range(feats):
                to_t, to_r, to_f = move(t, r, f)
                pairs.append(
                    (
                        (t * reps + r) * feats + f,
                        ((to_t % teams) * reps + to_r) * feats + to_f,
                    )
                )
    return pairs


def along_ring(value):
    return lax.ppermute(value, AXES, permutation(lambda t, r, f: (t + 1 - 2 * r, r, f)))


def between_cores(value):
    return lax.ppermute(value, AXES, permutation(lambda t, r, f: (t, 1 - r, f)))


def between_feats(value):
    return lax.ppermute(value, AXES, permutation(lambda t, r, f: (t, r, 1 - f)))


def after(value, first):
    return lax.optimization_barrier((value, first))


def in_vmem(value):
    return pltpu.with_memory_space_constraint(value, pltpu.VMEM)


def in_hbm(value):
    return pltpu.with_memory_space_constraint(value, pltpu.HBM)


ON_CHIP = pl.BlockSpec(memory_space=pltpu.VMEM)
SCALARS = pl.BlockSpec(memory_space=pltpu.SMEM)
OFF_CHIP = pl.BlockSpec(memory_space=pltpu.HBM)
COST = pl.CostEstimate(flops=0, bytes_accessed=0, transcendentals=0)
PARTS = 1
OWN, NEAR, NEAR_OTHER, FAR, FAR_OTHER, KEPT, GIVEN, COLUMNS = range(8)
PARAMS = pltpu.CompilerParams(vmem_limit_bytes=VMEM_LIMIT)


def part_kernel(first, count, feats, out, held, sem):
    rows = out.shape[0]
    copy = pltpu.make_async_copy(feats.at[pl.ds(first, rows)], held, sem)
    copy.start()
    copy.wait()
    row = lax.broadcasted_iota(jnp.int32, held.shape, 0) + first
    out[...] = jnp.where(row < count[0], held[...], jnp.zeros_like(held))


def part_of_slab(node_feats, node_count, first, rows):
    shape = (rows, node_feats.shape[1])
    return pl.pallas_call(
        functools.partial(part_kernel, first),
        out_shape=pltpu.VMEM(shape, node_feats.dtype),
        in_specs=[SCALARS, OFF_CHIP],
        out_specs=ON_CHIP,
        scratch_shapes=[
            pltpu.VMEM(shape, node_feats.dtype),
            pltpu.SemaphoreType.DMA,
        ],
        compiler_params=PARAMS,
        cost_estimate=COST,
        name="part_of_slab",
    )(node_count, in_hbm(node_feats))


def place_slab(slab, panels, size):
    at = 0
    for piece in slab:
        rows = piece.shape[0]
        panels[at : at + rows, :] = piece[...]
        at += rows
    panels[at:, :] = jnp.zeros((size, panels.shape[1]), panels.dtype)


def fetch(info, steps, tiles, targets, sems):
    copies = []
    for j, step in enumerate(steps):
        source, target = tiles.at[:, 0, info[step]], targets.at[j]
        count = target.shape[0] // PARTS
        for i in range(PARTS):
            run = pl.ds(i * count, count)
            copies.append(
                pltpu.make_async_copy(source.at[run], target.at[run], sems.at[j, i])
            )
    for copy in copies:
        copy.start()
    return copies


def product_kernel(step, index, fetched, ahead, halves, info, head, tail, *refs):
    refs, panels = refs[:-1], refs[-1]
    held, tiles, total = None, None, None
    if not fetched:
        held, held_sems, refs = refs[-2], refs[-1], refs[:-2]
    if ahead:
        ahead_sems, refs = refs[-1], refs[:-1]
        later, refs = refs[-1], refs[:-1]
    outs, refs = (refs[-2:], refs[:-2]) if halves else (refs[-1:], refs[:-1])
    if fetched:
        held, refs = refs[0], refs[1:]
    if ahead or not fetched:
        tiles, refs = refs[0], refs[1:]
    if refs:
        (total,) = refs
    _, groups, slots, size, _ = held.shape
    copies = [] if fetched else fetch(info, [step], tiles, held, held_sems)
    ahead_copies = fetch(info, ahead, tiles, later, ahead_sems) if ahead else []
    place_slab((head, tail), panels, size)
    for copy in copies:
        copy.wait()
    table = COLUMNS + info[step] * (groups * slots)
    for out, start_at in zip(outs, (GIVEN, KEPT)):
        start = info[start_at] if halves else 0
        for i in range(out.shape[0]):
            g = start + i
            lhs, rhs = [], []
            for k in range(slots):
                panel = info[table + g * slots + k]
                rows = pl.ds(pl.multiple_of(panel * size, size), size)
                lhs.append(held[index, g, k])
                rhs.append(panels[rows, :])
            value = jnp.dot(
                jnp.concatenate(lhs, axis=1),
                jnp.concatenate(rhs, axis=0),
                preferred_element_type=jnp.float32,
            )
            if total is not None:
                value = value + total[g]
            out[i] = value.astype(out.dtype)
    for copy in ahead_copies:
        copy.wait()


def product(step, info, slab, tiles, total, fetched=None, index=0, ahead=(), halves=False):
    groups, _, _, slots, size, _ = tiles.shape
    rows, width = sum(piece.shape[0] for piece in slab), slab[0].shape[1]
    operands, specs = [info, *map(in_vmem, slab)], [SCALARS, ON_CHIP, ON_CHIP]
    if halves:
        out_shape = [
            pltpu.VMEM((groups // 2, size, width), dtype)
            for dtype in (jnp.bfloat16, jnp.float32)
        ]
    else:
        out_shape = [pltpu.VMEM((groups, size, width), jnp.float32)]
    scratch = []
    if fetched is not None:
        operands.append(in_vmem(fetched))
        specs.append(ON_CHIP)
    if ahead or fetched is None:
        operands.append(in_hbm(tiles))
        specs.append(OFF_CHIP)
    if total is not None:
        operands.append(in_vmem(total))
        specs.append(ON_CHIP)
    if ahead:
        shape = (len(ahead), groups, slots, size, size)
        out_shape.append(pltpu.VMEM(shape, tiles.dtype))
        scratch.append(pltpu.SemaphoreType.DMA((len(ahead), PARTS)))
    if fetched is None:
        scratch.append(pltpu.VMEM((1, groups, slots, size, size), tiles.dtype))
        scratch.append(pltpu.SemaphoreType.DMA((1, PARTS)))
    scratch.append(pltpu.VMEM((rows + size, width), slab[0].dtype))
    outs = pl.pallas_call(
        functools.partial(
            product_kernel, step, index, fetched is not None, tuple(ahead), halves
        ),
        out_shape=out_shape,
        in_specs=specs,
        out_specs=[ON_CHIP] * len(out_shape),
        scratch_shapes=scratch,
        compiler_params=PARAMS,
        cost_estimate=COST,
        name="product",
    )(*operands)
    return outs if len(outs) > 1 else outs[0]


def add_kernel(kept, got, out):
    out[...] = (kept[...] + got[...].astype(jnp.float32)).astype(out.dtype)


def add(kept, got):
    return pl.pallas_call(
        add_kernel,
        out_shape=pltpu.VMEM(got.shape, got.dtype),
        in_specs=[ON_CHIP, ON_CHIP],
        out_specs=ON_CHIP,
        compiler_params=PARAMS,
        name="add_halves",
    )(in_vmem(kept), in_vmem(got))


def finish_kernel(place, count, agg, weight, bias, *refs):
    out, held, sems = refs[-3:]
    groups, size, _ = agg.shape
    rep, feat = place[0], place[1]
    live = count[0] - rep * (2 * groups * size)
    biased = bias[...].astype(jnp.float32)
    row = lax.broadcasted_iota(jnp.int32, held.shape[1:], 0)
    copies = []
    for g in range(groups):
        start = (2 * g + feat) * size
        value = jnp.dot(agg[g], weight[...], preferred_element_type=jnp.float32)
        value = jnp.maximum(value + biased, 0.0)
        held[g] = jnp.where(row + start < live, value, 0.0).astype(out.dtype)
        target = out.at[pl.ds(pl.multiple_of(start, size), size)]
        copies.append(pltpu.make_async_copy(held.at[g], target, sems.at[g]))
        copies[-1].start()
    for copy in copies:
        copy.wait()


def finish(place, count, agg, weight, bias, out=None):
    groups, size, _ = agg.shape
    share = weight.shape[1]
    before = [] if out is None else [out]
    return pl.pallas_call(
        finish_kernel,
        out_shape=jax.ShapeDtypeStruct((groups * 2 * size, share), agg.dtype),
        in_specs=[SCALARS, SCALARS] + [ON_CHIP] * 3 + [OFF_CHIP] * len(before),
        out_specs=OFF_CHIP,
        scratch_shapes=[
            pltpu.VMEM((groups, size, share), agg.dtype),
            pltpu.SemaphoreType.DMA((groups,)),
        ],
        input_output_aliases={5: 0} if before else {},
        compiler_params=PARAMS,
        name="finish",
    )(place, count, in_vmem(agg), in_vmem(weight), in_vmem(bias), *before)


def local(node_feats, tile_vals, tile_cols, tile_count, node_count, weight, bias):
    size = tile_vals.shape[-1]
    groups, _, spans, slots = tile_vals.shape[:4]
    reach = spans // 2
    rep, feat = lax.axis_index("rep"), lax.axis_index("feat")
    panels = node_feats.shape[0] // size
    slot_ids = rep * slots + jnp.arange(slots, dtype=jnp.int32)
    live = slot_ids[None, None, :] < tile_count[:, 0, :, None]
    columns = jnp.where(live, tile_cols[:, 0], panels)
    columns = columns.transpose(1, 0, 2).reshape(-1)
    half = groups // 2
    sign = 2 * rep - 1
    steps = reach + sign * jnp.array([0, 1, -1, 2, -2], jnp.int32)
    starts = jnp.stack([rep * half, (1 - rep) * half])
    info = jnp.concatenate([steps, starts, columns]).astype(jnp.int32)
    share = weight.shape[1] // lax.axis_size("feat")
    weight_own = lax.dynamic_slice_in_dim(weight, feat * share, share, 1)
    bias_own = lax.dynamic_slice_in_dim(bias, feat * share, share, 0)[None]

    rows = node_feats.shape[0]
    cut = rows * 5 // 8 // size * size
    own = [
        part_of_slab(node_feats, node_count, 0, cut),
        part_of_slab(node_feats, node_count, cut, rows - cut),
    ]
    near = [along_ring(piece) for piece in own]
    total, tiles = product(OWN, info, own, tile_vals, None, ahead=(NEAR, NEAR_OTHER))
    first, (total, tiles) = after(near[0], (total, tiles))
    near = [first, near[1]]
    far = [along_ring(piece) for piece in near]
    near_other = [between_cores(piece) for piece in near]
    total, far_tiles = product(
        NEAR, info, near, tile_vals, total, tiles, 0, ahead=(FAR, FAR_OTHER)
    )
    total = product(NEAR_OTHER, info, near_other, tile_vals, total, tiles, 1)
    far, (total, far_tiles) = after(far, (total, far_tiles))
    far_other = [between_cores(piece) for piece in far]
    total = product(FAR, info, far, tile_vals, total, far_tiles, 0)
    given, kept = product(
        FAR_OTHER, info, far_other, tile_vals, total, far_tiles, 1, halves=True
    )
    got = between_cores(given)
    mine = add(kept, got)
    theirs = between_feats(mine)
    here = jnp.stack([rep, feat]).astype(jnp.int32)
    there = jnp.stack([rep, 1 - feat]).astype(jnp.int32)
    out = finish(here, node_count, mine, weight_own, bias_own)
    return finish(there, node_count, theirs, weight_own, bias_own, out)


def solution(mesh):
    return jax.shard_map(
        local,
        mesh=mesh,
        in_specs=(
            P("team", None),
            P("team", "feat", None, "rep", None, None),
            P("team", "feat", None, "rep"),
            P("team", "feat", None),
            P("team"),
            P(),
            P(),
        ),
        out_specs=P(("team", "rep"), "feat"),
        check_vma=False,
    )
```

time: 208 us -> 56.4 us (0.27)
  waiting for transfers between devices: 108 us -> 9.56 us
  local copies, waits for them, and re-layouts: 23 us -> 0.98 us
  matrix products: 17.7 us -> 0 us
  Pallas kernels: 0 us -> 16.4 us
  between operations: 14.2 us -> 0.8 us
  blocking collectives: 10.3 us -> 0 us
  other arithmetic: 9.53 us -> 1.59 us
    ppermute x5 -> x10, waiting for transfers between devices: 89.7 us -> 9.56 us  [the longest x1 4.76 us: between_feats(): return lax.ppermute(value, AXES, permutation(lambda t, r, f: (t, r, 1 - f)))]
    reduce_scatter x1 -> x0, waiting for transfers between devices: 18.1 us -> none  [local(): summed = lax.psum_scatter(total, 'rep', scatter_dimension=0, tiled=True)]
    dot_general x6 -> x0, matrix products: 17.7 us -> none  [the longest x5 17.4 us: contribute(): jnp.einsum('gsij,gsjc->gic', tile_now, picked, preferred_element_type=jnp...]
    pallas_call x0 -> x10, Pallas kernels: none -> 16.4 us  [the longest x5 11 us: product(): pl.pallas_call(functools.partial(product_kernel, step, index, fetched is...]
    unnamed x9 -> x5, local copies, waits for them, and re-layouts: 14.1 us -> 0.69 us
    all_gather x1 -> x0, blocking collectives: 10.3 us -> none  [local(): lax.all_gather(own_agg[:, None], 'feat', axis=1, tiled=True)]
    gather x6 -> x0, local copies, waits for them, and re-layouts: 7.68 us -> none  [contribute(): panels[cols_now]]
    select_n x6 -> x0, other arithmetic: 6.8 us -> none  [the longest x5 3.42 us: contribute(): panels[cols_now]]
  transfers between devices with their start and end apart: 6 -> 10, of which waited for: 6 -> 4; matrix products, arithmetic and copies ran while one was open for 8% -> 5% of each run, Pallas kernels for 0% -> 22%
where the time goes in v1:
time: 56.4 us; the launch traced here: 56.1 us
  starting transfers between devices  26.8 us (48%)
  Pallas kernels  16.4 us (29%)
  waiting for transfers between devices  9.56 us (17%)
  other arithmetic  1.59 us (3%)
  local copies, waits for them, and re-layouts  0.98 us (2%)
  between operations  0.8 us (1%)
    ppermute x4, starting transfers between devices, along_ring(): lax.ppermute(value, AXES, permutation(lambda t, r, f: (t + 1 - 2 * r, r,...  18.6 us
    pallas_call x5, Pallas kernels, product(): pl.pallas_call(functools.partial(product_kernel, step, index, fetched is...  11 us
    ppermute x5, starting transfers between devices, between_cores(): return lax.ppermute(value, AXES, permutation(lambda t, r, f: (t, 1 - r, f)))  5.49 us
    ppermute x1, waiting for transfers between devices, between_feats(): return lax.ppermute(value, AXES, permutation(lambda t, r, f: (t, r, 1 - f)))  4.76 us
    pallas_call x2, Pallas kernels, finish(): pl.pallas_call(finish_kernel, out_shape=jax.ShapeDtypeStruct((groups * 2...  2.94 us
    ppermute x4, waiting for transfers between devices, along_ring(): lax.ppermute(value, AXES, permutation(lambda t, r, f: (t + 1 - 2 * r, r,...  2.71 us
    ppermute x1, starting transfers between devices, between_feats(): return lax.ppermute(value, AXES, permutation(lambda t, r, f: (t, r, 1 - f)))  2.71 us
    pallas_call x2, Pallas kernels, part_of_slab(): pl.pallas_call(functools.partial(part_kernel, first), out_shape=pltpu.VME...  2.39 us
  transfers between devices with their start and end apart: 10, of which 4 were waited for; matrix products, arithmetic and copies ran while one was open for 5% of the time, Pallas kernels for 22%

profile of v1, /device:TPU:1, one launch (start us, length us, event | category | flops | bytes accessed | tf_op | source)
XLA Modules:
  0.0 56.1 jit_solution(14349432149293787867)
XLA Ops:
  0.7 1.3 %part_of_slab.2.head = bf16[2560,128]{1,0:T(8,128)(2,1)S(1)} custom-call(s32[1]{0:T(128)S(6)} %copy.15.count, bf16[4096,128]{1,0:T(8,128)(2,1)} %feats.3), custom_call_target="tpu_custom_call" | custom-call | tf_op jit(solution)/shard_map/part_of_slab/pallas_call | solution.py:74
  2.0 9.7 %collective-permute-start = (bf16[2560,128]{1,0:T(8,128)(2,1)S(1)}, bf16[2560,128]{1,0:T(8,128)(2,1)S(1)}, u32[]{:S(2)}, u32[]{:S(2)}) collective-permute-start(bf16[2560,128]{1,0:T(8,128)(2,1)S(1)} %part_of_slab.2.head), channel_id=1, source_target_pairs={{0,4},{1,5},{2,254},{3,255},{4,8},{5,9},{6,2},{7,3},{8,12},{9,13},... | collective-permute-start | bytes 1966088 | tf_op jit(solution)/shard_map/ppermute | solution.py:31
  11.7 1.1 %part_of_slab.3.tail = bf16[1536,128]{1,0:T(8,128)(2,1)S(1)} custom-call(s32[1]{0:T(128)S(6)} %copy.15.count, bf16[4096,128]{1,0:T(8,128)(2,1)} %feats.3), custom_call_target="tpu_custom_call" | custom-call | tf_op jit(solution)/shard_map/part_of_slab/pallas_call | solution.py:74
  12.8 0.6 %collective-permute-start.2 = (bf16[1536,128]{1,0:T(8,128)(2,1)S(1)}, bf16[1536,128]{1,0:T(8,128)(2,1)S(1)}, u32[]{:S(2)}, u32[]{:S(2)}) collective-permute-start(bf16[1536,128]{1,0:T(8,128)(2,1)S(1)} %part_of_slab.3.tail), channel_id=1, source_target_pairs={{0,4},{1,5},{2,254},{3,255},{4,8},{5,9},{6,2},{7,3},{8,12},{9,13},... | collective-permute-start | bytes 1179656 | tf_op jit(solution)/shard_map/ppermute | solution.py:31
  13.4 0.7 %copy.13 = s32[16,1,5]{0,2,1:T(8,128)S(1)} copy(s32[16,1,5]{0,1,2:T(1,128)} %param.11) | data formatting | bytes 640
  14.1 0.8 %fusion = s32[5,16,4]{1,2,0:T(4,128)S(1)} fusion(s32[16,1,5,4]{0,3,2,1:T(4,128)} %param.10, s32[16,5]{0,1:T(8,128)S(1)} %bitcast.16, s32[4]{0:T(128)S(1)} %iota_add_fusion), kind=kLoop, calls=%fused_computation.1 | loop fusion | flops 640 | bytes 2896 | tf_op jit(solution)/shard_map/transpose | solution.py:264
  14.9 0.7 %multiply_add_fusion = s32[5]{0:T(128)S(1)} fusion(s32[5]{0:T(128)} %constant.27.clone, s32[]{:T(128)S(6)} %sub.10), kind=kLoop, calls=%fused_computation.8 | loop fusion | flops 10 | bytes 44 | tf_op jit(solution)/shard_map/add | solution.py:267
  15.8 3.5 %product.5 = (f32[16,128,128]{2,1,0:T(8,128)S(1)}, bf16[2,16,4,128,128]{4,3,2,1,0:T(8,128)(2,1)S(1)}) custom-call(s32[327]{0:T(512)S(1)} %pad_add_fusion.info, bf16[2560,128]{1,0:T(8,128)(2,1)S(1)} %part_of_slab.2.head, bf16[1536,128]{1,0:T(8,128)(2,1)S(1)} %part_of_slab.3.tail, bf16[16,1,5,4,128,128]{5,4,3,2,1,0:T(8,128)(2,1)} %refs_1_.1), custom_call_target="tpu_custom_call" | custom-call | tf_op jit(solution)/shard_map/product/pallas_call | solution.py:186
  19.4 1.8 %collective-permute-start.4 = (bf16[2560,128]{1,0:T(8,128)(2,1)S(1)}, bf16[2560,128]{1,0:T(8,128)(2,1)S(1)}, u32[]{:S(2)}, u32[]{:S(2)}) collective-permute-start(bf16[2560,128]{1,0:T(8,128)(2,1)S(1)} %collective-permute-done.head), channel_id=1, source_target_pairs={{0,2},{1,3},{2,0},{3,1},{4,6},{5,7},{6,4},{7,5},{8,10},{9,11},{10,... | collective-permute-start | bytes 1966088 | tf_op jit(solution)/shard_map/ppermute | solution.py:35
  21.2 4.1 %collective-permute-start.1 = (bf16[2560,128]{1,0:T(8,128)(2,1)S(1)}, bf16[2560,128]{1,0:T(8,128)(2,1)S(1)}, u32[]{:S(2)}, u32[]{:S(2)}) collective-permute-start(bf16[2560,128]{1,0:T(8,128)(2,1)S(1)} %collective-permute-done.head), channel_id=1, source_target_pairs={{0,4},{1,5},{2,254},{3,255},{4,8},{5,9},{6,2},{7,3},{8,12},{9,13},... | collective-permute-start | bytes 1966088 | tf_op jit(solution)/shard_map/ppermute | solution.py:31
  25.4 4.1 %collective-permute-start.3 = (bf16[1536,128]{1,0:T(8,128)(2,1)S(1)}, bf16[1536,128]{1,0:T(8,128)(2,1)S(1)}, u32[]{:S(2)}, u32[]{:S(2)}) collective-permute-start(bf16[1536,128]{1,0:T(8,128)(2,1)S(1)} %collective-permute-done.2.tail), channel_id=1, source_target_pairs={{0,4},{1,5},{2,254},{3,255},{4,8},{5,9},{6,2},{7,3},{8,12},{9,13},... | collective-permute-start | bytes 1179656 | tf_op jit(solution)/shard_map/ppermute | solution.py:31
  29.5 3.4 %product.6 = (f32[16,128,128]{2,1,0:T(8,128)S(1)}, bf16[2,16,4,128,128]{4,3,2,1,0:T(8,128)(2,1)S(1)}) custom-call(s32[327]{0:T(512)S(1)} %pad_add_fusion.info, bf16[2560,128]{1,0:T(8,128)(2,1)S(1)} %collective-permute-done.head, bf16[1536,128]{1,0:T(8,128)(2,1)S(1)} %collective-permute-done.2.tail, ...), custom_call_target="tpu_custom_call" | custom-call | tf_op jit(solution)/shard_map/product/pallas_call | solution.py:186
  33.0 1.4 %product.7.refs_1_ = f32[16,128,128]{2,1,0:T(8,128)S(1)} custom-call(s32[327]{0:T(512)S(1)} %pad_add_fusion.info, bf16[2560,128]{1,0:T(8,128)(2,1)S(1)} %collective-permute-done.4.head, bf16[1536,128]{1,0:T(8,128)(2,1)S(1)} %collective-permute-done.5.tail, bf16[2,16,4,128,128]{4,3,2,1,0:T(8,128)(2,1)S(1)} %get-tuple-element.21.refs_0_, ...), custom_call_target="tpu_custom_call" | custom-call | tf_op jit(solution)/shard_map/product/pallas_call | solution.py:186
  34.4 2.7 %collective-permute-done.3.tail = bf16[1536,128]{1,0:T(8,128)(2,1)S(1)} collective-permute-done((bf16[1536,128]{1,0:T(8,128)(2,1)S(1)}, bf16[1536,128]{1,0:T(8,128)(2,1)S(1)}, u32[]{:S(2)}, u32[]{:S(2)}) %collective-permute-start.3) | collective-permute-done | bytes 393248 | tf_op jit(solution)/shard_map/ppermute | solution.py:31
  37.1 3.1 %collective-permute-start.6 = (bf16[2560,128]{1,0:T(8,128)(2,1)S(1)}, bf16[2560,128]{1,0:T(8,128)(2,1)S(1)}, u32[]{:S(2)}, u32[]{:S(2)}) collective-permute-start(bf16[2560,128]{1,0:T(8,128)(2,1)S(1)} %collective-permute-done.1.head), channel_id=1, source_target_pairs={{0,2},{1,3},{2,0},{3,1},{4,6},{5,7},{6,4},{7,5},{8,10},{9,11},{10,... | collective-permute-start | bytes 1966088 | tf_op jit(solution)/shard_map/ppermute | solution.py:35
  40.2 1.4 %product.8.refs_1_ = f32[16,128,128]{2,1,0:T(8,128)S(1)} custom-call(s32[327]{0:T(512)S(1)} %pad_add_fusion.info, bf16[2560,128]{1,0:T(8,128)(2,1)S(1)} %collective-permute-done.1.head, bf16[1536,128]{1,0:T(8,128)(2,1)S(1)} %collective-permute-done.3.tail, bf16[2,16,4,128,128]{4,3,2,1,0:T(8,128)(2,1)S(1)} %get-tuple-element.27.refs_0_, ...), custom_call_target="tpu_custom_call" | custom-call | tf_op jit(solution)/shard_map/product/pallas_call | solution.py:186
  41.6 0.9 %collective-permute-done.7.tail = bf16[1536,128]{1,0:T(8,128)(2,1)S(1)} collective-permute-done((bf16[1536,128]{1,0:T(8,128)(2,1)S(1)}, bf16[1536,128]{1,0:T(8,128)(2,1)S(1)}, u32[]{:S(2)}, u32[]{:S(2)}) %collective-permute-start.7) | collective-permute-done | bytes 393248 | tf_op jit(solution)/shard_map/ppermute | solution.py:35
  42.5 1.4 %product.9 = (bf16[8,128,128]{2,1,0:T(8,128)(2,1)S(1)}, f32[8,128,128]{2,1,0:T(8,128)S(1)}) custom-call(s32[327]{0:T(512)S(1)} %pad_add_fusion.info, bf16[2560,128]{1,0:T(8,128)(2,1)S(1)} %collective-permute-done.6.head, bf16[1536,128]{1,0:T(8,128)(2,1)S(1)} %collective-permute-done.7.tail, bf16[2,16,4,128,128]{4,3,2,1,0:T(8,128)(2,1)S(1)} %get-tuple-element.27.refs_0_, ...), custom_call_target="tpu_custom_call" | custom-call | tf_op jit(solution)/shard_map/product/pallas_call | solution.py:186
  43.9 0.5 collective-permute-start.8
  44.3 1.2 %collective-permute-done.8.got = bf16[8,128,128]{2,1,0:T(8,128)(2,1)S(1)} collective-permute-done((bf16[8,128,128]{2,1,0:T(8,128)(2,1)S(1)}, bf16[8,128,128]{2,1,0:T(8,128)(2,1)S(1)}, u32[]{:S(2)}, u32[]{:S(2)}) %collective-permute-start.8) | collective-permute-done | bytes 262176 | tf_op jit(solution)/shard_map/ppermute | solution.py:35
  45.5 2.7 %collective-permute-start.9 = (bf16[8,128,128]{2,1,0:T(8,128)(2,1)S(1)}, bf16[8,128,128]{2,1,0:T(8,128)(2,1)S(1)}, u32[]{:S(2)}, u32[]{:S(2)}) collective-permute-start(bf16[8,128,128]{2,1,0:T(8,128)(2,1)S(1)} %add_halves.1.agg), channel_id=1, source_target_pairs={{0,1},{1,0},{2,3},{3,2},{4,5},{5,4},{6,7},{7,6},{8,9},{9,8},{10,11... | collective-permute-start | bytes 786440 | tf_op jit(solution)/shard_map/ppermute | solution.py:39
  48.4 1.5 %finish.2.refs_0_ = bf16[2048,128]{1,0:T(8,128)(2,1)} custom-call(s32[2]{0:T(128)S(1)} %get-tuple-element.32.place, s32[1]{0:T(128)S(6)} %copy.15.count, bf16[8,128,128]{2,1,0:T(8,128)(2,1)S(1)} %add_halves.1.agg, bf16[128,128]{1,0:T(8,128)(2,1)S(1)} %constant_dynamic-slice_fusion.weight, bf16[1,128]{1,0:T(2,128)(2,1)S(1)} %dynamic-slice_bitcast_fusion.bias), custom_call_target="tpu_custom_call" | custom-call | tf_op jit(solution)/shard_map/finish/pallas_call | solution.py:240
  49.9 4.8 %collective-permute-done.9.agg = bf16[8,128,128]{2,1,0:T(8,128)(2,1)S(1)} collective-permute-done((bf16[8,128,128]{2,1,0:T(8,128)(2,1)S(1)}, bf16[8,128,128]{2,1,0:T(8,128)(2,1)S(1)}, u32[]{:S(2)}, u32[]{:S(2)}) %collective-permute-start.9) | collective-permute-done | bytes 262176 | tf_op jit(solution)/shard_map/ppermute | solution.py:39
  54.6 1.5 %finish.3 = bf16[2048,128]{1,0:T(8,128)(2,1)} custom-call(s32[2]{0:T(128)S(1)} %get-tuple-element.31.place, s32[1]{0:T(128)S(6)} %copy.15.count, bf16[8,128,128]{2,1,0:T(8,128)(2,1)S(1)} %collective-permute-done.9.agg, bf16[128,128]{1,0:T(8,128)(2,1)S(1)} %constant_dynamic-slice_fusion.weight, ...), custom_call_target="tpu_custom_call", output_to_operand_aliasing={{}: (5, {})} | custom-call | tf_op jit(solution)/shard_map/finish/pallas_call | solution.py:240
  (20 shorter events, 0.6 us)
Async XLA Ops:
  0.0 48.4 %copy-start = (bf16[128,256]{1,0:T(8,128)(2,1)S(1)}, bf16[128,256]{1,0:T(8,128)(2,1)}, u32[]{:S(2)}) copy-start(bf16[128,256]{1,0:T(8,128)(2,1)} %param.13) | copy-start | bytes 196612
  2.0 17.4 %collective-permute-start = (bf16[2560,128]{1,0:T(8,128)(2,1)S(1)}, bf16[2560,128]{1,0:T(8,128)(2,1)S(1)}, u32[]{:S(2)}, u32[]{:S(2)}) collective-permute-start(bf16[2560,128]{1,0:T(8,128)(2,1)S(1)} %part_of_slab.2.head), channel_id=1, source_target_pairs={{0,4},{1,5},{2,254},{3,255},{4,8},{5,9},{6,2},{7,3},{8,12},{9,13},... | collective-permute-start | bytes 1966088 | tf_op jit(solution)/shard_map/ppermute | solution.py:31
  12.8 12.5 %collective-permute-start.2 = (bf16[1536,128]{1,0:T(8,128)(2,1)S(1)}, bf16[1536,128]{1,0:T(8,128)(2,1)S(1)}, u32[]{:S(2)}, u32[]{:S(2)}) collective-permute-start(bf16[1536,128]{1,0:T(8,128)(2,1)S(1)} %part_of_slab.3.tail), channel_id=1, source_target_pairs={{0,4},{1,5},{2,254},{3,255},{4,8},{5,9},{6,2},{7,3},{8,12},{9,13},... | collective-permute-start | bytes 1179656 | tf_op jit(solution)/shard_map/ppermute | solution.py:31
  19.4 13.6 %collective-permute-start.4 = (bf16[2560,128]{1,0:T(8,128)(2,1)S(1)}, bf16[2560,128]{1,0:T(8,128)(2,1)S(1)}, u32[]{:S(2)}, u32[]{:S(2)}) collective-permute-start(bf16[2560,128]{1,0:T(8,128)(2,1)S(1)} %collective-permute-done.head), channel_id=1, source_target_pairs={{0,2},{1,3},{2,0},{3,1},{4,6},{5,7},{6,4},{7,5},{8,10},{9,11},{10,... | collective-permute-start | bytes 1966088 | tf_op jit(solution)/shard_map/ppermute | solution.py:35
  21.2 15.9 %collective-permute-start.1 = (bf16[2560,128]{1,0:T(8,128)(2,1)S(1)}, bf16[2560,128]{1,0:T(8,128)(2,1)S(1)}, u32[]{:S(2)}, u32[]{:S(2)}) collective-permute-start(bf16[2560,128]{1,0:T(8,128)(2,1)S(1)} %collective-permute-done.head), channel_id=1, source_target_pairs={{0,4},{1,5},{2,254},{3,255},{4,8},{5,9},{6,2},{7,3},{8,12},{9,13},... | collective-permute-start | bytes 1966088 | tf_op jit(solution)/shard_map/ppermute | solution.py:31
  25.3 7.7 %collective-permute-start.5 = (bf16[1536,128]{1,0:T(8,128)(2,1)S(1)}, bf16[1536,128]{1,0:T(8,128)(2,1)S(1)}, u32[]{:S(2)}, u32[]{:S(2)}) collective-permute-start(bf16[1536,128]{1,0:T(8,128)(2,1)S(1)} %collective-permute-done.2.tail), channel_id=1, source_target_pairs={{0,2},{1,3},{2,0},{3,1},{4,6},{5,7},{6,4},{7,5},{8,10},{9,11},{10,... | collective-permute-start | bytes 1179656 | tf_op jit(solution)/shard_map/ppermute | solution.py:35
  25.4 11.7 %collective-permute-start.3 = (bf16[1536,128]{1,0:T(8,128)(2,1)S(1)}, bf16[1536,128]{1,0:T(8,128)(2,1)S(1)}, u32[]{:S(2)}, u32[]{:S(2)}) collective-permute-start(bf16[1536,128]{1,0:T(8,128)(2,1)S(1)} %collective-permute-done.2.tail), channel_id=1, source_target_pairs={{0,4},{1,5},{2,254},{3,255},{4,8},{5,9},{6,2},{7,3},{8,12},{9,13},... | collective-permute-start | bytes 1179656 | tf_op jit(solution)/shard_map/ppermute | solution.py:31
  37.1 5.4 %collective-permute-start.6 = (bf16[2560,128]{1,0:T(8,128)(2,1)S(1)}, bf16[2560,128]{1,0:T(8,128)(2,1)S(1)}, u32[]{:S(2)}, u32[]{:S(2)}) collective-permute-start(bf16[2560,128]{1,0:T(8,128)(2,1)S(1)} %collective-permute-done.1.head), channel_id=1, source_target_pairs={{0,2},{1,3},{2,0},{3,1},{4,6},{5,7},{6,4},{7,5},{8,10},{9,11},{10,... | collective-permute-start | bytes 1966088 | tf_op jit(solution)/shard_map/ppermute | solution.py:35
  40.2 2.3 %collective-permute-start.7 = (bf16[1536,128]{1,0:T(8,128)(2,1)S(1)}, bf16[1536,128]{1,0:T(8,128)(2,1)S(1)}, u32[]{:S(2)}, u32[]{:S(2)}) collective-permute-start(bf16[1536,128]{1,0:T(8,128)(2,1)S(1)} %collective-permute-done.3.tail), channel_id=1, source_target_pairs={{0,2},{1,3},{2,0},{3,1},{4,6},{5,7},{6,4},{7,5},{8,10},{9,11},{10,... | collective-permute-start | bytes 1179656 | tf_op jit(solution)/shard_map/ppermute | solution.py:35
  41.6 6.7 %copy-start.1 = (bf16[256]{0:T(256)(128)(2,1)S(1)}, bf16[256]{0:T(256)(128)(2,1)}, u32[]{:S(2)}) copy-start(bf16[256]{0:T(256)(128)(2,1)} %param.14) | copy-start | bytes 1540
  43.9 1.6 %collective-permute-start.8 = (bf16[8,128,128]{2,1,0:T(8,128)(2,1)S(1)}, bf16[8,128,128]{2,1,0:T(8,128)(2,1)S(1)}, u32[]{:S(2)}, u32[]{:S(2)}) collective-permute-start(bf16[8,128,128]{2,1,0:T(8,128)(2,1)S(1)} %get-tuple-element.30), channel_id=1, source_target_pairs={{0,2},{1,3},{2,0},{3,1},{4,6},{5,7},{6,4},{7,5},{8,10},{9,11},{10,... | collective-permute-start | bytes 786440 | tf_op jit(solution)/shard_map/ppermute | solution.py:35
  45.5 9.1 %collective-permute-start.9 = (bf16[8,128,128]{2,1,0:T(8,128)(2,1)S(1)}, bf16[8,128,128]{2,1,0:T(8,128)(2,1)S(1)}, u32[]{:S(2)}, u32[]{:S(2)}) collective-permute-start(bf16[8,128,128]{2,1,0:T(8,128)(2,1)S(1)} %add_halves.1.agg), channel_id=1, source_target_pairs={{0,1},{1,0},{2,3},{3,2},{4,5},{5,4},{6,7},{7,6},{8,9},{9,8},{10,11... | collective-permute-start | bytes 786440 | tf_op jit(solution)/shard_map/ppermute | solution.py:39

commit v2 on v1

v2 whole, which is shorter than its diff:
```python
import functools

import jax
import jax.numpy as jnp
from jax import lax
from jax.experimental import pallas as pl
from jax.experimental.pallas import tpu as pltpu
from jax.sharding import PartitionSpec as P

AXES = ("team", "rep", "feat")
VMEM_LIMIT = 24 * 1024 * 1024


def permutation(move):
    teams, reps, feats = (lax.axis_size(a) for a in AXES)
    pairs = []
    for t in range(teams):
        for r in range(reps):
            for f in range(feats):
                to_t, to_r, to_f = move(t, r, f)
                pairs.append(
                    (
                        (t * reps + r) * feats + f,
                        ((to_t % teams) * reps + to_r) * feats + to_f,
                    )
                )
    return pairs


def along_ring(value):
    return lax.ppermute(value, AXES, permutation(lambda t, r, f: (t + 1 - 2 * r, r, f)))


def between_cores(value):
    return lax.ppermute(value, AXES, permutation(lambda t, r, f: (t, 1 - r, f)))


def between_feats(value):
    return lax.ppermute(value, AXES, permutation(lambda t, r, f: (t, r, 1 - f)))


def after(value, first):
    return lax.optimization_barrier((value, first))


def in_vmem(value):
    return pltpu.with_memory_space_constraint(value, pltpu.VMEM)


def in_hbm(value):
    return pltpu.with_memory_space_constraint(value, pltpu.HBM)


ON_CHIP = pl.BlockSpec(memory_space=pltpu.VMEM)
SCALARS = pl.BlockSpec(memory_space=pltpu.SMEM)
OFF_CHIP = pl.BlockSpec(memory_space=pltpu.HBM)
COST = pl.CostEstimate(flops=0, bytes_accessed=0, transcendentals=0)
OWN, NEAR, NEAR_OTHER, FAR, FAR_OTHER = range(5)
PARAMS = pltpu.CompilerParams(vmem_limit_bytes=VMEM_LIMIT)


def head_kernel(feats, out, sem):
    copy = pltpu.make_async_copy(feats.at[pl.ds(0, out.shape[0])], out, sem)
    copy.start()
    copy.wait()


def tail_kernel(first, count, feats, out, held, sem):
    rows = out.shape[0]
    copy = pltpu.make_async_copy(feats.at[pl.ds(first, rows)], held, sem)
    copy.start()
    copy.wait()
    row = lax.broadcasted_iota(jnp.int32, held.shape, 0) + first
    out[...] = jnp.where(row < count[0:1, :], held[...], jnp.zeros_like(held))


def split(node_feats, count):
    rows, width = node_feats.shape
    half = (rows // 2, width)
    out = pltpu.VMEM(half, node_feats.dtype)
    options = dict(
        out_shape=out,
        out_specs=ON_CHIP,
        compiler_params=PARAMS,
        cost_estimate=COST,
    )
    node_feats = in_hbm(node_feats)
    head = pl.pallas_call(
        head_kernel,
        in_specs=[OFF_CHIP],
        scratch_shapes=[pltpu.SemaphoreType.DMA],
        name="head_of_slab",
        **options,
    )(node_feats)
    tail = pl.pallas_call(
        functools.partial(tail_kernel, rows // 2),
        in_specs=[ON_CHIP, OFF_CHIP],
        scratch_shapes=[out, pltpu.SemaphoreType.DMA],
        name="tail_of_slab",
        **options,
    )(in_vmem(count), node_feats)
    return [head, tail]


def thirds_kernel(head, tail, *outs):
    at, cut = 0, head.shape[0]
    for out in outs:
        end = at + out.shape[0]
        middle = min(max(cut, at), end)
        if middle > at:
            out[: middle - at] = head[at:middle]
        if end > middle:
            out[middle - at :] = tail[middle - cut : end - cut]
        at = end


def thirds(slab, size):
    rows, width = sum(piece.shape[0] for piece in slab), slab[0].shape[1]
    less = rows // 3 // size * size
    outs = [
        pltpu.VMEM((count, width), slab[0].dtype)
        for count in (rows - 2 * less, less, less)
    ]
    return pl.pallas_call(
        thirds_kernel,
        out_shape=outs,
        in_specs=[ON_CHIP] * 2,
        out_specs=[ON_CHIP] * 3,
        compiler_params=PARAMS,
        cost_estimate=COST,
        name="thirds",
    )(*map(in_vmem, slab))


def place_slab(slab, panels, size):
    at = 0
    for piece in slab:
        rows = piece.shape[0]
        panels[at : at + rows, :] = piece[...]
        at += rows
    panels[at:, :] = jnp.zeros((size, panels.shape[1]), panels.dtype)


def offset_of(step, spans):
    sign = 2 * lax.axis_index("rep") - 1
    return spans // 2 + sign * (0, 1, -1, 2, -2)[step]


def fetch(steps, tiles, targets, sems):
    copies = []
    for j, (step, target) in enumerate(zip(steps, targets)):
        source = tiles.at[:, 0, offset_of(step, tiles.shape[2])]
        copies.append(pltpu.make_async_copy(source, target, sems.at[j]))
    for copy in copies:
        copy.start()
    return copies


def product_kernel(step, fetched, ahead, halves, pieces, spans, columns, *refs):
    refs = list(refs)
    slab = [refs.pop(0) for _ in range(pieces)]
    held = refs.pop(0) if fetched else None
    total = refs.pop(0) if fetched else None
    tiles = refs.pop(0) if ahead or not fetched else None
    outs = [refs.pop(0) for _ in range(2 if halves else 1)]
    later = [refs.pop(0) for _ in ahead]
    panels = refs.pop(0)
    copies = []
    if not fetched:
        held, held_sems = refs.pop(0), refs.pop(0)
        copies = fetch([step], tiles, [held], held_sems)
    ahead_copies = fetch(ahead, tiles, later, refs.pop(0)) if ahead else []
    groups, slots, size, _ = held.shape
    place_slab(slab, panels, size)
    for copy in copies:
        copy.wait()
    table = offset_of(step, spans) * (groups * slots)
    rep = lax.axis_index("rep")
    for out, part in zip(outs, (1 - rep, rep)):
        start = part * (groups // 2) if halves else 0
        for i in range(out.shape[0]):
            g = start + i
            lhs, rhs = [], []
            for k in range(slots):
                panel = columns[table + g * slots + k]
                rows = pl.ds(pl.multiple_of(panel * size, size), size)
                lhs.append(held[g, k])
                rhs.append(panels[rows, :])
            value = jnp.dot(
                jnp.concatenate(lhs, axis=1),
                jnp.concatenate(rhs, axis=0),
                preferred_element_type=jnp.float32,
            )
            if fetched:
                value = value + total[g]
            out[i] = value.astype(out.dtype)
    for copy in ahead_copies:
        copy.wait()


def product(step, columns, slab, tiles, held=None, total=None, ahead=(), halves=False):
    groups, _, spans, slots, size, _ = tiles.shape
    rows, width = sum(piece.shape[0] for piece in slab), slab[0].shape[1]
    fetched = held is not None
    shape = (groups, slots, size, size)
    operands = [columns, *map(in_vmem, slab)]
    specs = [SCALARS] + [ON_CHIP] * len(slab)
    if halves:
        out_shape = [
            pltpu.VMEM((groups // 2, size, width), dtype)
            for dtype in (jnp.bfloat16, jnp.float32)
        ]
    else:
        out_shape = [pltpu.VMEM((groups, size, width), jnp.float32)]
    scratch = [pltpu.VMEM((rows + size, width), slab[0].dtype)]
    if fetched:
        operands += [in_vmem(held), in_vmem(total)]
        specs += [ON_CHIP] * 2
    else:
        scratch += [pltpu.VMEM(shape, tiles.dtype), pltpu.SemaphoreType.DMA((1,))]
    if ahead or not fetched:
        operands.append(in_hbm(tiles))
        specs.append(OFF_CHIP)
    if ahead:
        out_shape += [pltpu.VMEM(shape, tiles.dtype)] * len(ahead)
        scratch.append(pltpu.SemaphoreType.DMA((len(ahead),)))
    outs = pl.pallas_call(
        functools.partial(
            product_kernel, step, fetched, tuple(ahead), halves, len(slab), spans
        ),
        out_shape=out_shape,
        in_specs=specs,
        out_specs=[ON_CHIP] * len(out_shape),
        scratch_shapes=scratch,
        compiler_params=PARAMS,
        cost_estimate=COST,
        name="product",
    )(*operands)
    return outs if len(outs) > 1 else outs[0]


def add_kernel(kept, got, out):
    out[...] = (kept[...] + got[...].astype(jnp.float32)).astype(out.dtype)


def add(kept, got):
    return pl.pallas_call(
        add_kernel,
        out_shape=pltpu.VMEM(got.shape, got.dtype),
        in_specs=[ON_CHIP, ON_CHIP],
        out_specs=ON_CHIP,
        compiler_params=PARAMS,
        name="add_halves",
    )(in_vmem(kept), in_vmem(got))


def finish_kernel(other, count, agg, weight, bias, *refs):
    out, held, sem = refs[-3:]
    groups, size, _ = agg.shape
    feat = lax.axis_index("feat")
    feat = 1 - feat if other else feat
    live = count[0:1, :] - (lax.axis_index("rep") * (2 * groups) + feat) * size
    biased = bias[...].astype(jnp.float32)
    row = lax.broadcasted_iota(jnp.int32, held.shape[1:], 0)
    for g in range(groups):
        value = jnp.dot(agg[g], weight[...], preferred_element_type=jnp.float32)
        value = jnp.maximum(value + biased, 0.0)
        held[g] = jnp.where(row + 2 * g * size < live, value, 0.0).astype(out.dtype)
    copy = pltpu.make_async_copy(held, out.at[:, feat], sem)
    copy.start()
    copy.wait()


def finish(count, agg, weight, bias, out=None):
    groups, size, _ = agg.shape
    share = weight.shape[1]
    before = [] if out is None else [out]
    return pl.pallas_call(
        functools.partial(finish_kernel, out is not None),
        out_shape=jax.ShapeDtypeStruct((groups, 2, size, share), agg.dtype),
        in_specs=[ON_CHIP] * 4 + [OFF_CHIP] * len(before),
        out_specs=OFF_CHIP,
        scratch_shapes=[
            pltpu.VMEM((groups, size, share), agg.dtype),
            pltpu.SemaphoreType.DMA,
        ],
        input_output_aliases={4: 0} if before else {},
        compiler_params=PARAMS,
        name="finish",
    )(in_vmem(count), in_vmem(agg), in_vmem(weight), in_vmem(bias), *before)


def local(node_feats, tile_vals, tile_cols, tile_count, node_count, weight, bias):
    size = tile_vals.shape[-1]
    groups, _, spans, slots = tile_vals.shape[:4]
    reach = spans // 2
    rep, feat = lax.axis_index("rep"), lax.axis_index("feat")
    panels = node_feats.shape[0] // size
    slot_ids = rep * slots + jnp.arange(slots, dtype=jnp.int32)
    live = slot_ids[None, None, :] < tile_count[:, 0, :, None]
    columns = jnp.where(live, tile_cols[:, 0], panels)
    columns = columns.transpose(1, 0, 2).reshape(-1).astype(jnp.int32)
    share = weight.shape[1] // lax.axis_size("feat")
    weight_own = lax.dynamic_slice_in_dim(weight, feat * share, share, 1)
    bias_own = lax.dynamic_slice_in_dim(bias, feat * share, share, 0)[None]

    count = jnp.broadcast_to(node_count[None], (8, node_feats.shape[1]))
    own = split(node_feats, count)
    near = [along_ring(piece) for piece in own]
    total, near_tiles, near_other_tiles = product(
        OWN, columns, own, tile_vals, ahead=(NEAR, NEAR_OTHER)
    )
    first, (total, near_tiles, near_other_tiles) = after(
        near[0], (total, near_tiles, near_other_tiles)
    )
    near = [first, near[1]]
    far = [along_ring(piece) for piece in near]
    near_other = [between_cores(piece) for piece in thirds(near, size)]
    total, far_tiles, far_other_tiles = product(
        NEAR, columns, near, tile_vals, near_tiles, total, ahead=(FAR, FAR_OTHER)
    )
    total = product(NEAR_OTHER, columns, near_other, tile_vals, near_other_tiles, total)
    first, total = after(far[0], total)
    far = [first, far[1]]
    far_other = [between_cores(piece) for piece in far]
    total = product(FAR, columns, far, tile_vals, far_tiles, total)
    given, kept = product(
        FAR_OTHER, columns, far_other, tile_vals, far_other_tiles, total, halves=True
    )
    got = between_cores(given)
    mine = add(kept, got)
    theirs = between_feats(mine)
    out = finish(count, mine, weight_own, bias_own)
    out = finish(count, theirs, weight_own, bias_own, out)
    return out.reshape(-1, share)


def solution(mesh):
    return jax.shard_map(
        local,
        mesh=mesh,
        in_specs=(
            P("team", None),
            P("team", "feat", None, "rep", None, None),
            P("team", "feat", None, "rep"),
            P("team", "feat", None),
            P("team"),
            P(),
            P(),
        ),
        out_specs=P(("team", "rep"), "feat"),
        check_vma=False,
    )
```

time: 56.4 us -> 52.7 us (0.934)
  waiting for transfers between devices: 9.56 us -> 6.71 us
  starting transfers between devices: 26.8 us -> 29.4 us
  other arithmetic: 1.59 us -> 0.08 us
  Pallas kernels: 16.4 us -> 15.3 us
  local copies, waits for them, and re-layouts: 0.98 us -> 0.31 us
    ppermute x4, starting transfers between devices: 18.6 us -> 21.9 us  [along_ring(): lax.ppermute(value, AXES, permutation(lambda t, r, f: (t + 1 - 2 * r, r,...]
    ppermute x4, waiting for transfers between devices: 2.71 us -> 0.01 us  [along_ring(): lax.ppermute(value, AXES, permutation(lambda t, r, f: (t + 1 - 2 * r, r,...]
    pallas_call x9 -> x10, Pallas kernels: 16.4 us -> 15.2 us  [the longest x5 11 us: product(): pl.pallas_call(functools.partial(product_kernel, step, fetched, tuple(ahe...]
    ppermute x5 -> x6, waiting for transfers between devices: 2.08 us -> 1.34 us  [between_cores(): return lax.ppermute(value, AXES, permutation(lambda t, r, f: (t, 1 - r, f)))]
    ppermute x5 -> x6, starting transfers between devices: 5.49 us -> 4.77 us  [between_cores(): return lax.ppermute(value, AXES, permutation(lambda t, r, f: (t, 1 - r, f)))]
    transpose x1, other arithmetic: 0.77 us -> 0.07 us  [local(): columns = columns.transpose(1, 0, 2).reshape(-1).astype(jnp.int32)]
    unnamed x5 -> x9, local copies, waits for them, and re-layouts: 0.69 us -> 0.02 us
    add x1 -> x0, other arithmetic: 0.66 us -> none  [local(): steps = reach + sign * jnp.array([0, 1, -1, 2, -2], jnp.int32)]
  transfers between devices with their start and end apart: 10 -> 11, of which waited for: 4 -> 3; matrix products, arithmetic and copies ran while one was open for 5% -> 1% of each run, Pallas kernels for 22% -> 23%
where the time goes in v2:
time: 52.7 us; the launch traced here: 52.6 us
  starting transfers between devices  29.4 us (56%)
  Pallas kernels  15.3 us (29%)
  waiting for transfers between devices  6.71 us (13%)
  between operations  0.8 us (2%)
    ppermute x4, starting transfers between devices, along_ring(): lax.ppermute(value, AXES, permutation(lambda t, r, f: (t + 1 - 2 * r, r,...  21.9 us
    pallas_call x5, Pallas kernels, product(): pl.pallas_call(functools.partial(product_kernel, step, fetched, tuple(ahe...  11 us
    ppermute x1, waiting for transfers between devices, between_feats(): return lax.ppermute(value, AXES, permutation(lambda t, r, f: (t, r, 1 - f)))  5.36 us
    ppermute x6, starting transfers between devices, between_cores(): return lax.ppermute(value, AXES, permutation(lambda t, r, f: (t, 1 - r, f)))  4.77 us
    ppermute x1, starting transfers between devices, between_feats(): return lax.ppermute(value, AXES, permutation(lambda t, r, f: (t, r, 1 - f)))  2.71 us
    pallas_call x2, Pallas kernels, finish(): pl.pallas_call(functools.partial(finish_kernel, out is not None), out_sha...  1.89 us
    ppermute x6, waiting for transfers between devices, between_cores(): return lax.ppermute(value, AXES, permutation(lambda t, r, f: (t, 1 - r, f)))  1.34 us
    pallas_call x1, Pallas kernels, split(): pl.pallas_call(functools.partial(tail_kernel, rows // 2), in_specs=[ON_CH...  1.22 us
  transfers between devices with their start and end apart: 11, of which 3 were waited for; matrix products, arithmetic and copies ran while one was open for 1% of the time, Pallas kernels for 23%

profile of v2, /device:TPU:1, one launch (start us, length us, event | category | flops | bytes accessed | tf_op | source)
XLA Modules:
  0.0 52.6 jit_solution(3397768925626017018)
XLA Ops:
  0.0 1.1 %head_of_slab.1.refs_0_ = bf16[2048,128]{1,0:T(8,128)(2,1)S(1)} custom-call(bf16[4096,128]{1,0:T(8,128)(2,1)} %feats.3), custom_call_target="tpu_custom_call" | custom-call | tf_op jit(solution)/shard_map/head_of_slab/pallas_call | solution.py:88
  1.1 9.7 %collective-permute-start = (bf16[2048,128]{1,0:T(8,128)(2,1)S(1)}, bf16[2048,128]{1,0:T(8,128)(2,1)S(1)}, u32[]{:S(2)}, u32[]{:S(2)}) collective-permute-start(bf16[2048,128]{1,0:T(8,128)(2,1)S(1)} %head_of_slab.1.refs_0_), channel_id=1, source_target_pairs={{0,4},{1,5},{2,254},{3,255},{4,8},{5,9},{6,2},{7,3},{8,12},{9,13},... | collective-permute-start | bytes 1572872 | tf_op jit(solution)/shard_map/ppermute | solution.py:31
  11.5 1.2 %tail_of_slab.1.refs_1_ = bf16[2048,128]{1,0:T(8,128)(2,1)S(1)} custom-call(s32[8,128]{1,0:T(8,128)S(1)} %broadcast_in_dim.17.count, bf16[4096,128]{1,0:T(8,128)(2,1)} %feats.3), custom_call_target="tpu_custom_call" | custom-call | tf_op jit(solution)/shard_map/tail_of_slab/pallas_call | solution.py:95
  12.7 0.6 %collective-permute-start.2 = (bf16[2048,128]{1,0:T(8,128)(2,1)S(1)}, bf16[2048,128]{1,0:T(8,128)(2,1)S(1)}, u32[]{:S(2)}, u32[]{:S(2)}) collective-permute-start(bf16[2048,128]{1,0:T(8,128)(2,1)S(1)} %tail_of_slab.1.refs_1_), channel_id=1, source_target_pairs={{0,4},{1,5},{2,254},{3,255},{4,8},{5,9},{6,2},{7,3},{8,12},{9,13},... | collective-permute-start | bytes 1572872 | tf_op jit(solution)/shard_map/ppermute | solution.py:31
  13.4 0.1 copy.9
  13.5 0.1 reshape.12.columns
  13.6 3.5 %product.5 = (f32[16,128,128]{2,1,0:T(8,128)S(1)}, bf16[16,4,128,128]{3,2,1,0:T(8,128)(2,1)S(1)}, bf16[16,4,128,128]{3,2,1,0:T(8,128)(2,1)S(1)}) custom-call(s32[320]{0:T(512)S(1)} %reshape.12.columns, bf16[2048,128]{1,0:T(8,128)(2,1)S(1)} %head_of_slab.1.refs_0_, bf16[2048,128]{1,0:T(8,128)(2,1)S(1)} %tail_of_slab.1.refs_1_, ...), custom_call_target="tpu_custom_call" | custom-call | tf_op jit(solution)/shard_map/product/pallas_call | solution.py:227
  17.1 6.0 %collective-permute-start.1 = (bf16[2048,128]{1,0:T(8,128)(2,1)S(1)}, bf16[2048,128]{1,0:T(8,128)(2,1)S(1)}, u32[]{:S(2)}, u32[]{:S(2)}) collective-permute-start(bf16[2048,128]{1,0:T(8,128)(2,1)S(1)} %collective-permute-done.head.refs_0_), channel_id=1, source_target_pairs={{0,4},{1,5},{2,254},{3,255},{4,8},{5,9},{6,2},{7,3},{8,12},{9,13},... | collective-permute-start | bytes 1572872 | tf_op jit(solution)/shard_map/ppermute | solution.py:31
  23.0 5.6 %collective-permute-start.7 = (bf16[2048,128]{1,0:T(8,128)(2,1)S(1)}, bf16[2048,128]{1,0:T(8,128)(2,1)S(1)}, u32[]{:S(2)}, u32[]{:S(2)}) collective-permute-start(bf16[2048,128]{1,0:T(8,128)(2,1)S(1)} %collective-permute-done.2.tail.refs_1_), channel_id=1, source_target_pairs={{0,4},{1,5},{2,254},{3,255},{4,8},{5,9},{6,2},{7,3},{8,12},{9,13},... | collective-permute-start | bytes 1572872 | tf_op jit(solution)/shard_map/ppermute | solution.py:31
  28.8 0.5 collective-permute-start.4
  29.3 0.1 collective-permute-start.5
  29.4 3.5 %product.6 = (f32[16,128,128]{2,1,0:T(8,128)S(1)}, bf16[16,4,128,128]{3,2,1,0:T(8,128)(2,1)S(1)}, bf16[16,4,128,128]{3,2,1,0:T(8,128)(2,1)S(1)}) custom-call(s32[320]{0:T(512)S(1)} %reshape.12.columns, bf16[2048,128]{1,0:T(8,128)(2,1)S(1)} %collective-permute-done.head.refs_0_, bf16[2048,128]{1,0:T(8,128)(2,1)S(1)} %collective-permute-done.2.tail.refs_1_, ...), custom_call_target="tpu_custom_call" | custom-call | tf_op jit(solution)/shard_map/product/pallas_call | solution.py:227
  32.9 1.4 %product.7.refs_3_ = f32[16,128,128]{2,1,0:T(8,128)S(1)} custom-call(s32[320]{0:T(512)S(1)} %reshape.12.columns, bf16[1536,128]{1,0:T(8,128)(2,1)S(1)} %collective-permute-done.3.refs_0_, bf16[1280,128]{1,0:T(8,128)(2,1)S(1)} %collective-permute-done.4.refs_1_, bf16[1280,128]{1,0:T(8,128)(2,1)S(1)} %collective-permute-done.5.refs_2_, ...), custom_call_target="tpu_custom_call" | custom-call | tf_op jit(solution)/shard_map/product/pallas_call | solution.py:227
  34.3 0.5 collective-permute-start.6
  34.8 3.1 %collective-permute-start.8 = (bf16[2048,128]{1,0:T(8,128)(2,1)S(1)}, bf16[2048,128]{1,0:T(8,128)(2,1)S(1)}, u32[]{:S(2)}, u32[]{:S(2)}) collective-permute-start(bf16[2048,128]{1,0:T(8,128)(2,1)S(1)} %collective-permute-done.7.refs_1_), channel_id=1, source_target_pairs={{0,2},{1,3},{2,0},{3,1},{4,6},{5,7},{6,4},{7,5},{8,10},{9,11},{10,... | collective-permute-start | bytes 1572872 | tf_op jit(solution)/shard_map/ppermute | solution.py:35
  37.9 1.4 %product.8.refs_3_ = f32[16,128,128]{2,1,0:T(8,128)S(1)} custom-call(s32[320]{0:T(512)S(1)} %reshape.12.columns, bf16[2048,128]{1,0:T(8,128)(2,1)S(1)} %collective-permute-done.1.refs_0_, bf16[2048,128]{1,0:T(8,128)(2,1)S(1)} %collective-permute-done.7.refs_1_, bf16[16,4,128,128]{3,2,1,0:T(8,128)(2,1)S(1)} %get-tuple-element.35.refs_2_, ...), custom_call_target="tpu_custom_call" | custom-call | tf_op jit(solution)/shard_map/product/pallas_call | solution.py:227
  39.3 0.2 collective-permute-done.8.refs_1_
  39.5 1.4 %product.9 = (bf16[8,128,128]{2,1,0:T(8,128)(2,1)S(1)}, f32[8,128,128]{2,1,0:T(8,128)S(1)}) custom-call(s32[320]{0:T(512)S(1)} %reshape.12.columns, bf16[2048,128]{1,0:T(8,128)(2,1)S(1)} %collective-permute-done.6.refs_0_, bf16[2048,128]{1,0:T(8,128)(2,1)S(1)} %collective-permute-done.8.refs_1_, bf16[16,4,128,128]{3,2,1,0:T(8,128)(2,1)S(1)} %get-tuple-element.34.refs_2_, ...), custom_call_target="tpu_custom_call" | custom-call | tf_op jit(solution)/shard_map/product/pallas_call | solution.py:227
  40.8 0.5 collective-permute-start.9
  41.3 1.2 %collective-permute-done.9.got = bf16[8,128,128]{2,1,0:T(8,128)(2,1)S(1)} collective-permute-done((bf16[8,128,128]{2,1,0:T(8,128)(2,1)S(1)}, bf16[8,128,128]{2,1,0:T(8,128)(2,1)S(1)}, u32[]{:S(2)}, u32[]{:S(2)}) %collective-permute-start.9) | collective-permute-done | bytes 262176 | tf_op jit(solution)/shard_map/ppermute | solution.py:35
  42.5 2.7 %collective-permute-start.10 = (bf16[8,128,128]{2,1,0:T(8,128)(2,1)S(1)}, bf16[8,128,128]{2,1,0:T(8,128)(2,1)S(1)}, u32[]{:S(2)}, u32[]{:S(2)}) collective-permute-start(bf16[8,128,128]{2,1,0:T(8,128)(2,1)S(1)} %add_halves.1.agg), channel_id=1, source_target_pairs={{0,1},{1,0},{2,3},{3,2},{4,5},{5,4},{6,7},{7,6},{8,9},{9,8},{10,11... | collective-permute-start | bytes 786440 | tf_op jit(solution)/shard_map/ppermute | solution.py:39
  45.3 0.9 %finish.2.refs_0_ = bf16[8,2,128,128]{3,2,1,0:T(8,128)(2,1)} custom-call(s32[8,128]{1,0:T(8,128)S(1)} %broadcast_in_dim.17.count, bf16[8,128,128]{2,1,0:T(8,128)(2,1)S(1)} %add_halves.1.agg, bf16[128,128]{1,0:T(8,128)(2,1)S(1)} %constant_dynamic-slice_fusion.weight, bf16[1,128]{1,0:T(2,128)(2,1)S(1)} %dynamic-slice_bitcast_fusion.bias), custom_call_target="tpu_custom_call" | custom-call | tf_op jit(solution)/shard_map/finish/pallas_call | solution.py:278
  46.3 5.4 %collective-permute-done.10.agg = bf16[8,128,128]{2,1,0:T(8,128)(2,1)S(1)} collective-permute-done((bf16[8,128,128]{2,1,0:T(8,128)(2,1)S(1)}, bf16[8,128,128]{2,1,0:T(8,128)(2,1)S(1)}, u32[]{:S(2)}, u32[]{:S(2)}) %collective-permute-start.10) | collective-permute-done | bytes 262176 | tf_op jit(solution)/shard_map/ppermute | solution.py:39
  51.6 0.9 %finish.3 = bf16[8,2,128,128]{3,2,1,0:T(8,128)(2,1)} custom-call(s32[8,128]{1,0:T(8,128)S(1)} %broadcast_in_dim.17.count, bf16[8,128,128]{2,1,0:T(8,128)(2,1)S(1)} %collective-permute-done.10.agg, bf16[128,128]{1,0:T(8,128)(2,1)S(1)} %constant_dynamic-slice_fusion.weight, ...), custom_call_target="tpu_custom_call", output_to_operand_aliasing={{}: (4, {})} | custom-call | tf_op jit(solution)/shard_map/finish/pallas_call | solution.py:278
  (25 shorter events, 0.4 us)
Async XLA Ops:
  0.0 45.3 %copy-start = (bf16[128,256]{1,0:T(8,128)(2,1)S(1)}, bf16[128,256]{1,0:T(8,128)(2,1)}, u32[]{:S(2)}) copy-start(bf16[128,256]{1,0:T(8,128)(2,1)} %param.12) | copy-start | bytes 196612
  0.0 13.3 %copy-start.2 = (s32[16,1,5]{0,1,2:T(1,128)S(1)}, s32[16,1,5]{0,1,2:T(1,128)}, u32[]{:S(2)}) copy-start(s32[16,1,5]{0,1,2:T(1,128)} %param.10) | copy-start | bytes 964
  0.0 13.3 %copy-start.1 = (s32[16,1,5,4]{0,3,2,1:T(4,128)S(1)}, s32[16,1,5,4]{0,3,2,1:T(4,128)}, u32[]{:S(2)}) copy-start(s32[16,1,5,4]{0,3,2,1:T(4,128)} %param.9) | copy-start | bytes 3844
  1.1 16.0 %collective-permute-start = (bf16[2048,128]{1,0:T(8,128)(2,1)S(1)}, bf16[2048,128]{1,0:T(8,128)(2,1)S(1)}, u32[]{:S(2)}, u32[]{:S(2)}) collective-permute-start(bf16[2048,128]{1,0:T(8,128)(2,1)S(1)} %head_of_slab.1.refs_0_), channel_id=1, source_target_pairs={{0,4},{1,5},{2,254},{3,255},{4,8},{5,9},{6,2},{7,3},{8,12},{9,13},... | collective-permute-start | bytes 1572872 | tf_op jit(solution)/shard_map/ppermute | solution.py:31
  12.7 10.4 %collective-permute-start.2 = (bf16[2048,128]{1,0:T(8,128)(2,1)S(1)}, bf16[2048,128]{1,0:T(8,128)(2,1)S(1)}, u32[]{:S(2)}, u32[]{:S(2)}) collective-permute-start(bf16[2048,128]{1,0:T(8,128)(2,1)S(1)} %tail_of_slab.1.refs_1_), channel_id=1, source_target_pairs={{0,4},{1,5},{2,254},{3,255},{4,8},{5,9},{6,2},{7,3},{8,12},{9,13},... | collective-permute-start | bytes 1572872 | tf_op jit(solution)/shard_map/ppermute | solution.py:31
  17.1 17.2 %collective-permute-start.1 = (bf16[2048,128]{1,0:T(8,128)(2,1)S(1)}, bf16[2048,128]{1,0:T(8,128)(2,1)S(1)}, u32[]{:S(2)}, u32[]{:S(2)}) collective-permute-start(bf16[2048,128]{1,0:T(8,128)(2,1)S(1)} %collective-permute-done.head.refs_0_), channel_id=1, source_target_pairs={{0,4},{1,5},{2,254},{3,255},{4,8},{5,9},{6,2},{7,3},{8,12},{9,13},... | collective-permute-start | bytes 1572872 | tf_op jit(solution)/shard_map/ppermute | solution.py:31
  23.0 11.8 %collective-permute-start.7 = (bf16[2048,128]{1,0:T(8,128)(2,1)S(1)}, bf16[2048,128]{1,0:T(8,128)(2,1)S(1)}, u32[]{:S(2)}, u32[]{:S(2)}) collective-permute-start(bf16[2048,128]{1,0:T(8,128)(2,1)S(1)} %collective-permute-done.2.tail.refs_1_), channel_id=1, source_target_pairs={{0,4},{1,5},{2,254},{3,255},{4,8},{5,9},{6,2},{7,3},{8,12},{9,13},... | collective-permute-start | bytes 1572872 | tf_op jit(solution)/shard_map/ppermute | solution.py:31
  28.7 4.2 %collective-permute-start.3 = (bf16[1536,128]{1,0:T(8,128)(2,1)S(1)}, bf16[1536,128]{1,0:T(8,128)(2,1)S(1)}, u32[]{:S(2)}, u32[]{:S(2)}) collective-permute-start(bf16[1536,128]{1,0:T(8,128)(2,1)S(1)} %get-tuple-element.26), channel_id=1, source_target_pairs={{0,2},{1,3},{2,0},{3,1},{4,6},{5,7},{6,4},{7,5},{8,10},{9,11},{10,... | collective-permute-start | bytes 1179656 | tf_op jit(solution)/shard_map/ppermute | solution.py:35
  28.8 4.1 %collective-permute-start.4 = (bf16[1280,128]{1,0:T(8,128)(2,1)S(1)}, bf16[1280,128]{1,0:T(8,128)(2,1)S(1)}, u32[]{:S(2)}, u32[]{:S(2)}) collective-permute-start(bf16[1280,128]{1,0:T(8,128)(2,1)S(1)} %get-tuple-element.27), channel_id=1, source_target_pairs={{0,2},{1,3},{2,0},{3,1},{4,6},{5,7},{6,4},{7,5},{8,10},{9,11},{10,... | collective-permute-start | bytes 983048 | tf_op jit(solution)/shard_map/ppermute | solution.py:35
  29.3 3.6 %collective-permute-start.5 = (bf16[1280,128]{1,0:T(8,128)(2,1)S(1)}, bf16[1280,128]{1,0:T(8,128)(2,1)S(1)}, u32[]{:S(2)}, u32[]{:S(2)}) collective-permute-start(bf16[1280,128]{1,0:T(8,128)(2,1)S(1)} %get-tuple-element.28), channel_id=1, source_target_pairs={{0,2},{1,3},{2,0},{3,1},{4,6},{5,7},{6,4},{7,5},{8,10},{9,11},{10,... | collective-permute-start | bytes 983048 | tf_op jit(solution)/shard_map/ppermute | solution.py:35
  34.3 5.0 %collective-permute-start.6 = (bf16[2048,128]{1,0:T(8,128)(2,1)S(1)}, bf16[2048,128]{1,0:T(8,128)(2,1)S(1)}, u32[]{:S(2)}, u32[]{:S(2)}) collective-permute-start(bf16[2048,128]{1,0:T(8,128)(2,1)S(1)} %collective-permute-done.1.refs_0_), channel_id=1, source_target_pairs={{0,2},{1,3},{2,0},{3,1},{4,6},{5,7},{6,4},{7,5},{8,10},{9,11},{10,... | collective-permute-start | bytes 1572872 | tf_op jit(solution)/shard_map/ppermute | solution.py:35
  34.8 4.7 %collective-permute-start.8 = (bf16[2048,128]{1,0:T(8,128)(2,1)S(1)}, bf16[2048,128]{1,0:T(8,128)(2,1)S(1)}, u32[]{:S(2)}, u32[]{:S(2)}) collective-permute-start(bf16[2048,128]{1,0:T(8,128)(2,1)S(1)} %collective-permute-done.7.refs_1_), channel_id=1, source_target_pairs={{0,2},{1,3},{2,0},{3,1},{4,6},{5,7},{6,4},{7,5},{8,10},{9,11},{10,... | collective-permute-start | bytes 1572872 | tf_op jit(solution)/shard_map/ppermute | solution.py:35
  39.5 5.7 %copy-start.3 = (bf16[256]{0:T(256)(128)(2,1)S(1)}, bf16[256]{0:T(256)(128)(2,1)}, u32[]{:S(2)}) copy-start(bf16[256]{0:T(256)(128)(2,1)} %param.13) | copy-start | bytes 1540
  40.8 1.6 %collective-permute-start.9 = (bf16[8,128,128]{2,1,0:T(8,128)(2,1)S(1)}, bf16[8,128,128]{2,1,0:T(8,128)(2,1)S(1)}, u32[]{:S(2)}, u32[]{:S(2)}) collective-permute-start(bf16[8,128,128]{2,1,0:T(8,128)(2,1)S(1)} %get-tuple-element.38), channel_id=1, source_target_pairs={{0,2},{1,3},{2,0},{3,1},{4,6},{5,7},{6,4},{7,5},{8,10},{9,11},{10,... | collective-permute-start | bytes 786440 | tf_op jit(solution)/shard_map/ppermute | solution.py:35
  42.5 9.1 %collective-permute-start.10 = (bf16[8,128,128]{2,1,0:T(8,128)(2,1)S(1)}, bf16[8,128,128]{2,1,0:T(8,128)(2,1)S(1)}, u32[]{:S(2)}, u32[]{:S(2)}) collective-permute-start(bf16[8,128,128]{2,1,0:T(8,128)(2,1)S(1)} %add_halves.1.agg), channel_id=1, source_target_pairs={{0,1},{1,0},{2,3},{3,2},{4,5},{5,4},{6,7},{7,6},{8,9},{9,8},{10,11... | collective-permute-start | bytes 786440 | tf_op jit(solution)/shard_map/ppermute | solution.py:39

commit v3 on v2

--- a/solution.py
+++ b/solution.py
@@ -29,6 +29,10 @@
 
 def along_ring(value):
     return lax.ppermute(value, AXES, permutation(lambda t, r, f: (t + 1 - 2 * r, r, f)))
+
+
+def further_along(value):
+    return lax.ppermute(value, AXES, permutation(lambda t, r, f: (t + 1 - 2 * r, 1 - r, f)))
 
 
 def between_cores(value):
@@ -143,7 +147,7 @@
 
 def offset_of(step, spans):
     sign = 2 * lax.axis_index("rep") - 1
-    return spans // 2 + sign * (0, 1, -1, 2, -2)[step]
+    return spans // 2 + sign * (0, 1, -1, -2, 2)[step]
 
 
 def fetch(steps, tiles, targets, sems):
@@ -156,35 +160,53 @@
     return copies
 
 
-def product_kernel(step, fetched, ahead, halves, pieces, spans, columns, *refs):
+def product_kernel(step, fetched, ahead, last, part, pieces, spans, columns, *refs):
     refs = list(refs)
     slab = [refs.pop(0) for _ in range(pieces)]
     held = refs.pop(0) if fetched else None
     total = refs.pop(0) if fetched else None
     tiles = refs.pop(0) if ahead or not fetched else None
-    outs = [refs.pop(0) for _ in range(2 if halves else 1)]
-    later = [refs.pop(0) for _ in ahead]
-    panels = refs.pop(0)
+    split_out = last and not ahead
+    outs = [refs.pop(0) for _ in range(2 if split_out else 1)]
+    later = [refs.pop(0) for _ in range(len(ahead) + (last and bool(ahead)))]
+    panels, table, table_sem = refs.pop(0), refs.pop(0), refs.pop(0)
+    table_copy = pltpu.make_async_copy(columns, table, table_sem)
+    table_copy.start()
+    rep = lax.axis_index("rep")
     copies = []
     if not fetched:
         held, held_sems = refs.pop(0), refs.pop(0)
         copies = fetch([step], tiles, [held], held_sems)
-    ahead_copies = fetch(ahead, tiles, later, refs.pop(0)) if ahead else []
-    groups, slots, size, _ = held.shape
+    ahead_copies = []
+    if ahead:
+        sems = refs.pop(0)
+        whole = ahead[:-1] if last else ahead
+        ahead_copies = fetch(whole, tiles, later, sems)
+        if last:
+            source = tiles.at[:, 0, offset_of(ahead[-1], spans)]
+            for i, target in enumerate(later[-2:]):
+                count = target.shape[0]
+                half = source.at[pl.ds((1 - rep, rep)[i] * count, count)]
+                sem = sems.at[len(whole) + i]
+                ahead_copies.append(pltpu.make_async_copy(half, target, sem))
+                ahead_copies[-1].start()
+    _, slots, size, _ = held.shape
+    groups = table.shape[0] // (spans * slots)
     place_slab(slab, panels, size)
+    table_copy.wait()
     for copy in copies:
         copy.wait()
-    table = offset_of(step, spans) * (groups * slots)
-    rep = lax.axis_index("rep")
-    for out, part in zip(outs, (1 - rep, rep)):
-        start = part * (groups // 2) if halves else 0
+    first = offset_of(step, spans) * (groups * slots)
+    for j, out in enumerate(outs):
+        halved = split_out or part is not None
+        start = (1 - rep, rep)[part or j] * (groups // 2) if halved else 0
         for i in range(out.shape[0]):
-            g = start + i
+            at = i if part is not None else start + i
             lhs, rhs = [], []
             for k in range(slots):
-                panel = columns[table + g * slots + k]
+                panel = table[first + (start + i) * slots + k]
                 rows = pl.ds(pl.multiple_of(panel * size, size), size)
-                lhs.append(held[g, k])
+                lhs.append(held[at, k])
                 rhs.append(panels[rows, :])
             value = jnp.dot(
                 jnp.concatenate(lhs, axis=1),
@@ -192,27 +214,34 @@
                 preferred_element_type=jnp.float32,
             )
             if fetched:
-                value = value + total[g]
+                value = value + total[at]
             out[i] = value.astype(out.dtype)
     for copy in ahead_copies:
         copy.wait()
 
 
-def product(step, columns, slab, tiles, held=None, total=None, ahead=(), halves=False):
+def product(
+    step, columns, slab, tiles, held=None, total=None, ahead=(), last=False, part=None
+):
     groups, _, spans, slots, size, _ = tiles.shape
     rows, width = sum(piece.shape[0] for piece in slab), slab[0].shape[1]
     fetched = held is not None
-    shape = (groups, slots, size, size)
+    shape, half = (groups, slots, size, size), (groups // 2, slots, size, size)
     operands = [columns, *map(in_vmem, slab)]
-    specs = [SCALARS] + [ON_CHIP] * len(slab)
-    if halves:
-        out_shape = [
-            pltpu.VMEM((groups // 2, size, width), dtype)
-            for dtype in (jnp.bfloat16, jnp.float32)
-        ]
-    else:
-        out_shape = [pltpu.VMEM((groups, size, width), jnp.float32)]
-    scratch = [pltpu.VMEM((rows + size, width), slab[0].dtype)]
+    specs = [pl.BlockSpec(memory_space=pl.ANY)] + [ON_CHIP] * len(slab)
+    sums = pltpu.VMEM((groups, size, width), jnp.float32)
+    half_sums = pltpu.VMEM((groups // 2, size, width), jnp.float32)
+    out_shape = [sums]
+    if part is not None:
+        dtype = (jnp.bfloat16, jnp.float32)[part]
+        out_shape = [pltpu.VMEM((groups // 2, size, width), dtype)]
+    elif last and not ahead:
+        out_shape = [half_sums] * 2
+    scratch = [
+        pltpu.VMEM((rows + size, width), slab[0].dtype),
+        pltpu.SMEM(columns.shape, columns.dtype),
+        pltpu.SemaphoreType.DMA,
+    ]
     if fetched:
         operands += [in_vmem(held), in_vmem(total)]
         specs += [ON_CHIP] * 2
@@ -222,11 +251,12 @@
         operands.append(in_hbm(tiles))
         specs.append(OFF_CHIP)
     if ahead:
-        out_shape += [pltpu.VMEM(shape, tiles.dtype)] * len(ahead)
-        scratch.append(pltpu.SemaphoreType.DMA((len(ahead),)))
+        later = [shape] * (len(ahead) - last) + [half] * (2 * last)
+        out_shape += [pltpu.VMEM(each, tiles.dtype) for each in later]
+        scratch.append(pltpu.SemaphoreType.DMA((len(later),)))
     outs = pl.pallas_call(
         functools.partial(
-            product_kernel, step, fetched, tuple(ahead), halves, len(slab), spans
+            product_kernel, step, fetched, tuple(ahead), last, part, len(slab), spans
         ),
         out_shape=out_shape,
         in_specs=specs,
@@ -314,18 +344,21 @@
         near[0], (total, near_tiles, near_other_tiles)
     )
     near = [first, near[1]]
-    far = [along_ring(piece) for piece in near]
+    far = [further_along(piece) for piece in near]
     near_other = [between_cores(piece) for piece in thirds(near, size)]
-    total, far_tiles, far_other_tiles = product(
-        NEAR, columns, near, tile_vals, near_tiles, total, ahead=(FAR, FAR_OTHER)
+    total, far_tiles, *far_other_tiles = product(
+        NEAR, columns, near, tile_vals, near_tiles, total, (FAR, FAR_OTHER), last=True
     )
     total = product(NEAR_OTHER, columns, near_other, tile_vals, near_other_tiles, total)
     first, total = after(far[0], total)
     far = [first, far[1]]
     far_other = [between_cores(piece) for piece in far]
-    total = product(FAR, columns, far, tile_vals, far_tiles, total)
-    given, kept = product(
-        FAR_OTHER, columns, far_other, tile_vals, far_other_tiles, total, halves=True
+    totals = product(FAR, columns, far, tile_vals, far_tiles, total, last=True)
+    given, kept = (
+        product(
+            FAR_OTHER, columns, far_other, tile_vals, far_other_tiles[i], totals[i], part=i
+        )
+        for i in range(2)
     )
     got = between_cores(given)
     mine = add(kept, got)

time: 52.7 us -> 50.4 us (0.956)
  starting transfers between devices: 29.4 us -> 21.7 us
  waiting for transfers between devices: 6.71 us -> 13.3 us
  Pallas kernels: 15.3 us -> 14.1 us
    ppermute x4 -> x2, starting transfers between devices: 21.9 us -> 10.3 us  [along_ring(): lax.ppermute(value, AXES, permutation(lambda t, r, f: (t + 1 - 2 * r, r,...]
    ppermute x0 -> x2, starting transfers between devices: none -> 7.23 us  [further_along(): lax.ppermute(value, AXES, permutation(lambda t, r, f: (t + 1 - 2 * r, 1 -...]
    ppermute x0 -> x2, waiting for transfers between devices: none -> 4.34 us  [further_along(): lax.ppermute(value, AXES, permutation(lambda t, r, f: (t + 1 - 2 * r, 1 -...]
    ppermute x6, starting transfers between devices: 4.77 us -> 1.41 us  [between_cores(): return lax.ppermute(value, AXES, permutation(lambda t, r, f: (t, 1 - r, f)))]
    ppermute x4 -> x2, waiting for transfers between devices: 0.01 us -> 2.4 us  [along_ring(): lax.ppermute(value, AXES, permutation(lambda t, r, f: (t + 1 - 2 * r, r,...]
    pallas_call x5 -> x6, Pallas kernels: 11 us -> 9.79 us  [product(): pl.pallas_call(functools.partial(product_kernel, step, fetched, tuple(ahe...]
  transfers between devices with their start and end apart: 11 -> 11, of which waited for: 3 -> 6; matrix products, arithmetic and copies ran while one was open for 1% -> 1% of each run, Pallas kernels for 23% -> 22%
where the time goes in v3:
time: 50.4 us; the launch traced here: 50.3 us
  starting transfers between devices  21.7 us (43%)
  Pallas kernels  14.1 us (28%)
  waiting for transfers between devices  13.3 us (26%)
  between operations  0.81 us (2%)
    ppermute x2, starting transfers between devices, along_ring(): lax.ppermute(value, AXES, permutation(lambda t, r, f: (t + 1 - 2 * r, r,...  10.3 us
    pallas_call x6, Pallas kernels, product(): pl.pallas_call(functools.partial(product_kernel, step, fetched, tuple(ahe...  9.79 us
    ppermute x2, starting transfers between devices, further_along(): lax.ppermute(value, AXES, permutation(lambda t, r, f: (t + 1 - 2 * r, 1 -...  7.23 us
    ppermute x1, waiting for transfers between devices, between_feats(): return lax.ppermute(value, AXES, permutation(lambda t, r, f: (t, r, 1 - f)))  5.61 us
    ppermute x2, waiting for transfers between devices, further_along(): lax.ppermute(value, AXES, permutation(lambda t, r, f: (t + 1 - 2 * r, 1 -...  4.34 us
    ppermute x1, starting transfers between devices, between_feats(): return lax.ppermute(value, AXES, permutation(lambda t, r, f: (t, r, 1 - f)))  2.71 us
    ppermute x2, waiting for transfers between devices, along_ring(): lax.ppermute(value, AXES, permutation(lambda t, r, f: (t + 1 - 2 * r, r,...  2.4 us
    pallas_call x2, Pallas kernels, finish(): pl.pallas_call(functools.partial(finish_kernel, out is not None), out_sha...  1.89 us
  transfers between devices with their start and end apart: 11, of which 6 were waited for; matrix products, arithmetic and copies ran while one was open for 1% of the time, Pallas kernels for 22%

profile of v3, /device:TPU:1, one launch (start us, length us, event | category | flops | bytes accessed | tf_op | source)
XLA Modules:
  0.0 50.3 jit_solution(7340434033978392034)
XLA Ops:
  0.0 1.1 %head_of_slab.1.refs_0_ = bf16[2048,128]{1,0:T(8,128)(2,1)S(1)} custom-call(bf16[4096,128]{1,0:T(8,128)(2,1)} %feats.3), custom_call_target="tpu_custom_call" | custom-call | tf_op jit(solution)/shard_map/head_of_slab/pallas_call | solution.py:92
  1.1 9.7 %collective-permute-start = (bf16[2048,128]{1,0:T(8,128)(2,1)S(1)}, bf16[2048,128]{1,0:T(8,128)(2,1)S(1)}, u32[]{:S(2)}, u32[]{:S(2)}) collective-permute-start(bf16[2048,128]{1,0:T(8,128)(2,1)S(1)} %head_of_slab.1.refs_0_), channel_id=1, source_target_pairs={{0,4},{1,5},{2,254},{3,255},{4,8},{5,9},{6,2},{7,3},{8,12},{9,13},... | collective-permute-start | bytes 1572872 | tf_op jit(solution)/shard_map/ppermute | solution.py:31
  11.5 1.2 %tail_of_slab.1.refs_1_ = bf16[2048,128]{1,0:T(8,128)(2,1)S(1)} custom-call(s32[8,128]{1,0:T(8,128)S(1)} %broadcast_in_dim.17.count, bf16[4096,128]{1,0:T(8,128)(2,1)} %feats.3), custom_call_target="tpu_custom_call" | custom-call | tf_op jit(solution)/shard_map/tail_of_slab/pallas_call | solution.py:99
  12.7 0.6 %collective-permute-start.2 = (bf16[2048,128]{1,0:T(8,128)(2,1)S(1)}, bf16[2048,128]{1,0:T(8,128)(2,1)S(1)}, u32[]{:S(2)}, u32[]{:S(2)}) collective-permute-start(bf16[2048,128]{1,0:T(8,128)(2,1)S(1)} %tail_of_slab.1.refs_1_), channel_id=1, source_target_pairs={{0,4},{1,5},{2,254},{3,255},{4,8},{5,9},{6,2},{7,3},{8,12},{9,13},... | collective-permute-start | bytes 1572872 | tf_op jit(solution)/shard_map/ppermute | solution.py:31
  13.6 2.9 %product.6 = (f32[16,128,128]{2,1,0:T(8,128)S(1)}, bf16[16,4,128,128]{3,2,1,0:T(8,128)(2,1)S(1)}, bf16[16,4,128,128]{3,2,1,0:T(8,128)(2,1)S(1)}) custom-call(s32[320]{0:T(512)S(1)} %reshape.12.columns, bf16[2048,128]{1,0:T(8,128)(2,1)S(1)} %head_of_slab.1.refs_0_, bf16[2048,128]{1,0:T(8,128)(2,1)S(1)} %tail_of_slab.1.refs_1_, ...), custom_call_target="tpu_custom_call" | custom-call | tf_op jit(solution)/shard_map/product/pallas_call | solution.py:257
  16.5 0.4 collective-permute-done.head.refs_0_
  16.9 3.6 %collective-permute-start.1 = (bf16[2048,128]{1,0:T(8,128)(2,1)S(1)}, bf16[2048,128]{1,0:T(8,128)(2,1)S(1)}, u32[]{:S(2)}, u32[]{:S(2)}) collective-permute-start(bf16[2048,128]{1,0:T(8,128)(2,1)S(1)} %collective-permute-done.head.refs_0_), channel_id=1, source_target_pairs={{0,6},{1,7},{2,252},{3,253},{4,10},{5,11},{6,0},{7,1},{8,14},{9,15... | collective-permute-start | bytes 1572872 | tf_op jit(solution)/shard_map/ppermute | solution.py:35
  20.5 2.0 %collective-permute-done.2.tail.refs_1_ = bf16[2048,128]{1,0:T(8,128)(2,1)S(1)} collective-permute-done((bf16[2048,128]{1,0:T(8,128)(2,1)S(1)}, bf16[2048,128]{1,0:T(8,128)(2,1)S(1)}, u32[]{:S(2)}, u32[]{:S(2)}) %collective-permute-start.2) | collective-permute-done | bytes 524320 | tf_op jit(solution)/shard_map/ppermute | solution.py:31
  22.5 3.6 %collective-permute-start.7 = (bf16[2048,128]{1,0:T(8,128)(2,1)S(1)}, bf16[2048,128]{1,0:T(8,128)(2,1)S(1)}, u32[]{:S(2)}, u32[]{:S(2)}) collective-permute-start(bf16[2048,128]{1,0:T(8,128)(2,1)S(1)} %collective-permute-done.2.tail.refs_1_), channel_id=1, source_target_pairs={{0,6},{1,7},{2,252},{3,253},{4,10},{5,11},{6,0},{7,1},{8,14},{9,15... | collective-permute-start | bytes 1572872 | tf_op jit(solution)/shard_map/ppermute | solution.py:35
  26.3 0.5 collective-permute-start.4
  26.9 2.2 %product.7 = (f32[16,128,128]{2,1,0:T(8,128)S(1)}, bf16[16,4,128,128]{3,2,1,0:T(8,128)(2,1)S(1)}, bf16[8,4,128,128]{3,2,1,0:T(8,128)(2,1)S(1)}, bf16[8,4,128,128]{3,2,1,0:T(8,128)(2,1)S(1)}) custom-call(s32[320]{0:T(512)S(1)} %reshape.12.columns, bf16[2048,128]{1,0:T(8,128)(2,1)S(1)} %collective-permute-done.head.refs_0_, ...), custom_call_target="tpu_custom_call" | custom-call | tf_op jit(solution)/shard_map/product/pallas_call | solution.py:257
  29.2 1.3 %product.8.refs_3_ = f32[16,128,128]{2,1,0:T(8,128)S(1)} custom-call(s32[320]{0:T(512)S(1)} %reshape.12.columns, bf16[1536,128]{1,0:T(8,128)(2,1)S(1)} %collective-permute-done.3.refs_0_, bf16[1280,128]{1,0:T(8,128)(2,1)S(1)} %collective-permute-done.4.refs_1_, bf16[1280,128]{1,0:T(8,128)(2,1)S(1)} %collective-permute-done.5.refs_2_, ...), custom_call_target="tpu_custom_call" | custom-call | tf_op jit(solution)/shard_map/product/pallas_call | solution.py:257
  30.5 0.5 collective-permute-start.6
  31.0 4.3 %collective-permute-done.7.refs_1_ = bf16[2048,128]{1,0:T(8,128)(2,1)S(1)} collective-permute-done((bf16[2048,128]{1,0:T(8,128)(2,1)S(1)}, bf16[2048,128]{1,0:T(8,128)(2,1)S(1)}, u32[]{:S(2)}, u32[]{:S(2)}) %collective-permute-start.7) | collective-permute-done | bytes 524320 | tf_op jit(solution)/shard_map/ppermute | solution.py:35
  35.4 1.3 %product.9 = (f32[8,128,128]{2,1,0:T(8,128)S(1)}, f32[8,128,128]{2,1,0:T(8,128)S(1)}) custom-call(s32[320]{0:T(512)S(1)} %reshape.12.columns, bf16[2048,128]{1,0:T(8,128)(2,1)S(1)} %collective-permute-done.1.refs_0_, bf16[2048,128]{1,0:T(8,128)(2,1)S(1)} %collective-permute-done.7.refs_1_, bf16[16,4,128,128]{3,2,1,0:T(8,128)(2,1)S(1)} %get-tuple-element.36.refs_2_, ...), custom_call_target="tpu_custom_call" | custom-call | tf_op jit(solution)/shard_map/product/pallas_call | solution.py:257
  36.7 0.6 %collective-permute-done.8.refs_1_ = bf16[2048,128]{1,0:T(8,128)(2,1)S(1)} collective-permute-done((bf16[2048,128]{1,0:T(8,128)(2,1)S(1)}, bf16[2048,128]{1,0:T(8,128)(2,1)S(1)}, u32[]{:S(2)}, u32[]{:S(2)}) %collective-permute-start.8) | collective-permute-done | bytes 524320 | tf_op jit(solution)/shard_map/ppermute | solution.py:39
  37.3 1.0 %product.11 = bf16[8,128,128]{2,1,0:T(8,128)(2,1)S(1)} custom-call(s32[320]{0:T(512)S(1)} %reshape.12.columns, bf16[2048,128]{1,0:T(8,128)(2,1)S(1)} %collective-permute-done.6.refs_0_, bf16[2048,128]{1,0:T(8,128)(2,1)S(1)} %collective-permute-done.8.refs_1_, bf16[8,4,128,128]{3,2,1,0:T(8,128)(2,1)S(1)} %get-tuple-element.39.refs_2_, ...), custom_call_target="tpu_custom_call" | custom-call | tf_op jit(solution)/shard_map/product/pallas_call | solution.py:257
  38.3 0.2 collective-permute-start.9
  38.5 1.0 %product.10.kept = f32[8,128,128]{2,1,0:T(8,128)S(1)} custom-call(s32[320]{0:T(512)S(1)} %reshape.12.columns, bf16[2048,128]{1,0:T(8,128)(2,1)S(1)} %collective-permute-done.6.refs_0_, bf16[2048,128]{1,0:T(8,128)(2,1)S(1)} %collective-permute-done.8.refs_1_, bf16[8,4,128,128]{3,2,1,0:T(8,128)(2,1)S(1)} %get-tuple-element.35.refs_2_, ...), custom_call_target="tpu_custom_call" | custom-call | tf_op jit(solution)/shard_map/product/pallas_call | solution.py:257
  39.5 0.4 collective-permute-done.9.got
  40.0 2.7 %collective-permute-start.10 = (bf16[8,128,128]{2,1,0:T(8,128)(2,1)S(1)}, bf16[8,128,128]{2,1,0:T(8,128)(2,1)S(1)}, u32[]{:S(2)}, u32[]{:S(2)}) collective-permute-start(bf16[8,128,128]{2,1,0:T(8,128)(2,1)S(1)} %add_halves.1.agg), channel_id=1, source_target_pairs={{0,1},{1,0},{2,3},{3,2},{4,5},{5,4},{6,7},{7,6},{8,9},{9,8},{10,11... | collective-permute-start | bytes 786440 | tf_op jit(solution)/shard_map/ppermute | solution.py:43
  42.8 0.9 %finish.2.refs_0_ = bf16[8,2,128,128]{3,2,1,0:T(8,128)(2,1)} custom-call(s32[8,128]{1,0:T(8,128)S(1)} %broadcast_in_dim.17.count, bf16[8,128,128]{2,1,0:T(8,128)(2,1)S(1)} %add_halves.1.agg, bf16[128,128]{1,0:T(8,128)(2,1)S(1)} %constant_dynamic-slice_fusion.weight, bf16[1,128]{1,0:T(2,128)(2,1)S(1)} %dynamic-slice_bitcast_fusion.bias), custom_call_target="tpu_custom_call" | custom-call | tf_op jit(solution)/shard_map/finish/pallas_call | solution.py:308
  43.7 5.6 %collective-permute-done.10.agg = bf16[8,128,128]{2,1,0:T(8,128)(2,1)S(1)} collective-permute-done((bf16[8,128,128]{2,1,0:T(8,128)(2,1)S(1)}, bf16[8,128,128]{2,1,0:T(8,128)(2,1)S(1)}, u32[]{:S(2)}, u32[]{:S(2)}) %collective-permute-start.10) | collective-permute-done | bytes 262176 | tf_op jit(solution)/shard_map/ppermute | solution.py:43
  49.3 0.9 %finish.3 = bf16[8,2,128,128]{3,2,1,0:T(8,128)(2,1)} custom-call(s32[8,128]{1,0:T(8,128)S(1)} %broadcast_in_dim.17.count, bf16[8,128,128]{2,1,0:T(8,128)(2,1)S(1)} %collective-permute-done.10.agg, bf16[128,128]{1,0:T(8,128)(2,1)S(1)} %constant_dynamic-slice_fusion.weight, ...), custom_call_target="tpu_custom_call", output_to_operand_aliasing={{}: (4, {})} | custom-call | tf_op jit(solution)/shard_map/finish/pallas_call | solution.py:308
  (26 shorter events, 0.7 us)
Async XLA Ops:
  0.0 42.8 %copy-start = (bf16[128,256]{1,0:T(8,128)(2,1)S(1)}, bf16[128,256]{1,0:T(8,128)(2,1)}, u32[]{:S(2)}) copy-start(bf16[128,256]{1,0:T(8,128)(2,1)} %param.12) | copy-start | bytes 196612
  0.0 13.3 %copy-start.2 = (s32[16,1,5]{0,1,2:T(1,128)S(1)}, s32[16,1,5]{0,1,2:T(1,128)}, u32[]{:S(2)}) copy-start(s32[16,1,5]{0,1,2:T(1,128)} %param.10) | copy-start | bytes 964
  0.0 13.3 %copy-start.1 = (s32[16,1,5,4]{0,3,2,1:T(4,128)S(1)}, s32[16,1,5,4]{0,3,2,1:T(4,128)}, u32[]{:S(2)}) copy-start(s32[16,1,5,4]{0,3,2,1:T(4,128)} %param.9) | copy-start | bytes 3844
  1.1 15.8 %collective-permute-start = (bf16[2048,128]{1,0:T(8,128)(2,1)S(1)}, bf16[2048,128]{1,0:T(8,128)(2,1)S(1)}, u32[]{:S(2)}, u32[]{:S(2)}) collective-permute-start(bf16[2048,128]{1,0:T(8,128)(2,1)S(1)} %head_of_slab.1.refs_0_), channel_id=1, source_target_pairs={{0,4},{1,5},{2,254},{3,255},{4,8},{5,9},{6,2},{7,3},{8,12},{9,13},... | collective-permute-start | bytes 1572872 | tf_op jit(solution)/shard_map/ppermute | solution.py:31
  12.7 9.9 %collective-permute-start.2 = (bf16[2048,128]{1,0:T(8,128)(2,1)S(1)}, bf16[2048,128]{1,0:T(8,128)(2,1)S(1)}, u32[]{:S(2)}, u32[]{:S(2)}) collective-permute-start(bf16[2048,128]{1,0:T(8,128)(2,1)S(1)} %tail_of_slab.1.refs_1_), channel_id=1, source_target_pairs={{0,4},{1,5},{2,254},{3,255},{4,8},{5,9},{6,2},{7,3},{8,12},{9,13},... | collective-permute-start | bytes 1572872 | tf_op jit(solution)/shard_map/ppermute | solution.py:31
  16.9 13.6 %collective-permute-start.1 = (bf16[2048,128]{1,0:T(8,128)(2,1)S(1)}, bf16[2048,128]{1,0:T(8,128)(2,1)S(1)}, u32[]{:S(2)}, u32[]{:S(2)}) collective-permute-start(bf16[2048,128]{1,0:T(8,128)(2,1)S(1)} %collective-permute-done.head.refs_0_), channel_id=1, source_target_pairs={{0,6},{1,7},{2,252},{3,253},{4,10},{5,11},{6,0},{7,1},{8,14},{9,15... | collective-permute-start | bytes 1572872 | tf_op jit(solution)/shard_map/ppermute | solution.py:35
  22.5 12.8 %collective-permute-start.7 = (bf16[2048,128]{1,0:T(8,128)(2,1)S(1)}, bf16[2048,128]{1,0:T(8,128)(2,1)S(1)}, u32[]{:S(2)}, u32[]{:S(2)}) collective-permute-start(bf16[2048,128]{1,0:T(8,128)(2,1)S(1)} %collective-permute-done.2.tail.refs_1_), channel_id=1, source_target_pairs={{0,6},{1,7},{2,252},{3,253},{4,10},{5,11},{6,0},{7,1},{8,14},{9,15... | collective-permute-start | bytes 1572872 | tf_op jit(solution)/shard_map/ppermute | solution.py:35
  26.2 3.0 %collective-permute-start.3 = (bf16[1536,128]{1,0:T(8,128)(2,1)S(1)}, bf16[1536,128]{1,0:T(8,128)(2,1)S(1)}, u32[]{:S(2)}, u32[]{:S(2)}) collective-permute-start(bf16[1536,128]{1,0:T(8,128)(2,1)S(1)} %get-tuple-element.27), channel_id=1, source_target_pairs={{0,2},{1,3},{2,0},{3,1},{4,6},{5,7},{6,4},{7,5},{8,10},{9,11},{10,... | collective-permute-start | bytes 1179656 | tf_op jit(solution)/shard_map/ppermute | solution.py:39
  26.3 2.8 %collective-permute-start.4 = (bf16[1280,128]{1,0:T(8,128)(2,1)S(1)}, bf16[1280,128]{1,0:T(8,128)(2,1)S(1)}, u32[]{:S(2)}, u32[]{:S(2)}) collective-permute-start(bf16[1280,128]{1,0:T(8,128)(2,1)S(1)} %get-tuple-element.28), channel_id=1, source_target_pairs={{0,2},{1,3},{2,0},{3,1},{4,6},{5,7},{6,4},{7,5},{8,10},{9,11},{10,... | collective-permute-start | bytes 983048 | tf_op jit(solution)/shard_map/ppermute | solution.py:39
  26.8 2.3 %collective-permute-start.5 = (bf16[1280,128]{1,0:T(8,128)(2,1)S(1)}, bf16[1280,128]{1,0:T(8,128)(2,1)S(1)}, u32[]{:S(2)}, u32[]{:S(2)}) collective-permute-start(bf16[1280,128]{1,0:T(8,128)(2,1)S(1)} %get-tuple-element.29), channel_id=1, source_target_pairs={{0,2},{1,3},{2,0},{3,1},{4,6},{5,7},{6,4},{7,5},{8,10},{9,11},{10,... | collective-permute-start | bytes 983048 | tf_op jit(solution)/shard_map/ppermute | solution.py:39
  30.5 6.1 %collective-permute-start.6 = (bf16[2048,128]{1,0:T(8,128)(2,1)S(1)}, bf16[2048,128]{1,0:T(8,128)(2,1)S(1)}, u32[]{:S(2)}, u32[]{:S(2)}) collective-permute-start(bf16[2048,128]{1,0:T(8,128)(2,1)S(1)} %collective-permute-done.1.refs_0_), channel_id=1, source_target_pairs={{0,2},{1,3},{2,0},{3,1},{4,6},{5,7},{6,4},{7,5},{8,10},{9,11},{10,... | collective-permute-start | bytes 1572872 | tf_op jit(solution)/shard_map/ppermute | solution.py:39
  35.4 1.9 %collective-permute-start.8 = (bf16[2048,128]{1,0:T(8,128)(2,1)S(1)}, bf16[2048,128]{1,0:T(8,128)(2,1)S(1)}, u32[]{:S(2)}, u32[]{:S(2)}) collective-permute-start(bf16[2048,128]{1,0:T(8,128)(2,1)S(1)} %collective-permute-done.7.refs_1_), channel_id=1, source_target_pairs={{0,2},{1,3},{2,0},{3,1},{4,6},{5,7},{6,4},{7,5},{8,10},{9,11},{10,... | collective-permute-start | bytes 1572872 | tf_op jit(solution)/shard_map/ppermute | solution.py:39
  38.3 1.6 %collective-permute-start.9 = (bf16[8,128,128]{2,1,0:T(8,128)(2,1)S(1)}, bf16[8,128,128]{2,1,0:T(8,128)(2,1)S(1)}, u32[]{:S(2)}, u32[]{:S(2)}) collective-permute-start(bf16[8,128,128]{2,1,0:T(8,128)(2,1)S(1)} %product.11), channel_id=1, source_target_pairs={{0,2},{1,3},{2,0},{3,1},{4,6},{5,7},{6,4},{7,5},{8,10},{9,11},{10,... | collective-permute-start | bytes 786440 | tf_op jit(solution)/shard_map/ppermute | solution.py:39
  38.5 4.2 %copy-start.3 = (bf16[256]{0:T(256)(128)(2,1)S(1)}, bf16[256]{0:T(256)(128)(2,1)}, u32[]{:S(2)}) copy-start(bf16[256]{0:T(256)(128)(2,1)} %param.13) | copy-start | bytes 1540
  40.0 9.4 %collective-permute-start.10 = (bf16[8,128,128]{2,1,0:T(8,128)(2,1)S(1)}, bf16[8,128,128]{2,1,0:T(8,128)(2,1)S(1)}, u32[]{:S(2)}, u32[]{:S(2)}) collective-permute-start(bf16[8,128,128]{2,1,0:T(8,128)(2,1)S(1)} %add_halves.1.agg), channel_id=1, source_target_pairs={{0,1},{1,0},{2,3},{3,2},{4,5},{5,4},{6,7},{7,6},{8,9},{9,8},{10,11... | collective-permute-start | bytes 786440 | tf_op jit(solution)/shard_map/ppermute | solution.py:43

commit v4 on v2

--- a/solution.py
+++ b/solution.py
@@ -31,6 +31,10 @@
     return lax.ppermute(value, AXES, permutation(lambda t, r, f: (t + 1 - 2 * r, r, f)))
 
 
+def further_along(value):
+    return lax.ppermute(value, AXES, permutation(lambda t, r, f: (t + 1 - 2 * r, 1 - r, f)))
+
+
 def between_cores(value):
     return lax.ppermute(value, AXES, permutation(lambda t, r, f: (t, 1 - r, f)))
 
@@ -45,6 +49,10 @@
 
 def in_vmem(value):
     return pltpu.with_memory_space_constraint(value, pltpu.VMEM)
+
+
+def in_smem(value):
+    return pltpu.with_memory_space_constraint(value, pltpu.SMEM)
 
 
 def in_hbm(value):
@@ -56,6 +64,8 @@
 OFF_CHIP = pl.BlockSpec(memory_space=pltpu.HBM)
 COST = pl.CostEstimate(flops=0, bytes_accessed=0, transcendentals=0)
 OWN, NEAR, NEAR_OTHER, FAR, FAR_OTHER = range(5)
+GIVEN, KEPT = range(2)
+GIFTS = 2
 PARAMS = pltpu.CompilerParams(vmem_limit_bytes=VMEM_LIMIT)
 
 
@@ -143,90 +153,124 @@
 
 def offset_of(step, spans):
     sign = 2 * lax.axis_index("rep") - 1
-    return spans // 2 + sign * (0, 1, -1, 2, -2)[step]
-
-
-def fetch(steps, tiles, targets, sems):
-    copies = []
-    for j, (step, target) in enumerate(zip(steps, targets)):
-        source = tiles.at[:, 0, offset_of(step, tiles.shape[2])]
-        copies.append(pltpu.make_async_copy(source, target, sems.at[j]))
-    for copy in copies:
-        copy.start()
-    return copies
-
-
-def product_kernel(step, fetched, ahead, halves, pieces, spans, columns, *refs):
+    return spans // 2 + sign * (0, 1, -1, -2, 2)[step]
+
+
+def table_kernel(columns, out, sem):
+    copy = pltpu.make_async_copy(columns, out, sem)
+    copy.start()
+    copy.wait()
+
+
+def table_of(columns):
+    return pl.pallas_call(
+        table_kernel,
+        out_shape=pltpu.SMEM(columns.shape, columns.dtype),
+        in_specs=[pl.BlockSpec(memory_space=pl.ANY)],
+        out_specs=SCALARS,
+        scratch_shapes=[pltpu.SemaphoreType.DMA],
+        compiler_params=PARAMS,
+        cost_estimate=COST,
+        name="table",
+    )(columns)
+
+
+def terms(panels, table, first, slots, tiles, at):
+    size = tiles.shape[-1]
+    rhs = []
+    for k in range(slots):
+        rows = pl.ds(pl.multiple_of(table[first + k] * size, size), size)
+        rhs.append(panels[rows, :])
+    return [tiles[at, k] for k in range(slots)], rhs
+
+
+def multiplied(lhs, rhs):
+    return jnp.dot(
+        jnp.concatenate(lhs, axis=1),
+        jnp.concatenate(rhs, axis=0),
+        preferred_element_type=jnp.float32,
+    )
+
+
+def halves(groups):
+    rep = lax.axis_index("rep")
+    return (1 - rep) * (groups // 2), rep * (groups // 2)
+
+
+def product_kernel(step, fetched, ahead, parts, halved, pieces, spans, table, *refs):
     refs = list(refs)
     slab = [refs.pop(0) for _ in range(pieces)]
     held = refs.pop(0) if fetched else None
     total = refs.pop(0) if fetched else None
-    tiles = refs.pop(0) if ahead or not fetched else None
-    outs = [refs.pop(0) for _ in range(2 if halves else 1)]
+    tiles = refs.pop(0) if ahead or parts or not fetched else None
+    outs = [refs.pop(0) for _ in range(2 if halved else 1)]
     later = [refs.pop(0) for _ in ahead]
-    panels = refs.pop(0)
+    part_refs = [[refs.pop(0) for _ in range(runs)] for _, _, runs in parts]
+    panels, sems = refs.pop(0), refs.pop(0)
+    if not fetched:
+        held = refs.pop(0)
+    groups, slots, size, _ = held.shape
     copies = []
     if not fetched:
-        held, held_sems = refs.pop(0), refs.pop(0)
-        copies = fetch([step], tiles, [held], held_sems)
-    ahead_copies = fetch(ahead, tiles, later, refs.pop(0)) if ahead else []
-    groups, slots, size, _ = held.shape
+        copies.append((tiles.at[:, 0, offset_of(step, spans)], held))
+    now = len(copies)
+    for other, target in zip(ahead, later):
+        copies.append((tiles.at[:, 0, offset_of(other, spans)], target))
+    for (other, half, _), targets in zip(parts, part_refs):
+        for i, target in enumerate(targets):
+            count = target.shape[0]
+            run = pl.ds(halves(groups)[half] + i * count, count)
+            copies.append((tiles.at[run, 0, offset_of(other, spans)], target))
+    copies = [
+        pltpu.make_async_copy(source, target, sems.at[i])
+        for i, (source, target) in enumerate(copies)
+    ]
+    for copy in copies:
+        copy.start()
     place_slab(slab, panels, size)
-    for copy in copies:
+    for copy in copies[:now]:
         copy.wait()
-    table = offset_of(step, spans) * (groups * slots)
-    rep = lax.axis_index("rep")
-    for out, part in zip(outs, (1 - rep, rep)):
-        start = part * (groups // 2) if halves else 0
+    first = offset_of(step, spans) * (groups * slots)
+    for out, start in zip(outs, halves(groups) if halved else (0,)):
         for i in range(out.shape[0]):
             g = start + i
-            lhs, rhs = [], []
-            for k in range(slots):
-                panel = columns[table + g * slots + k]
-                rows = pl.ds(pl.multiple_of(panel * size, size), size)
-                lhs.append(held[g, k])
-                rhs.append(panels[rows, :])
-            value = jnp.dot(
-                jnp.concatenate(lhs, axis=1),
-                jnp.concatenate(rhs, axis=0),
-                preferred_element_type=jnp.float32,
-            )
+            value = multiplied(*terms(panels, table, first + g * slots, slots, held, g))
             if fetched:
                 value = value + total[g]
             out[i] = value.astype(out.dtype)
-    for copy in ahead_copies:
+    for copy in copies[now:]:
         copy.wait()
 
 
-def product(step, columns, slab, tiles, held=None, total=None, ahead=(), halves=False):
+def product(
+    step, table, slab, tiles, held=None, total=None, ahead=(), parts=(), halved=False
+):
     groups, _, spans, slots, size, _ = tiles.shape
     rows, width = sum(piece.shape[0] for piece in slab), slab[0].shape[1]
     fetched = held is not None
     shape = (groups, slots, size, size)
-    operands = [columns, *map(in_vmem, slab)]
+    operands = [in_smem(table), *map(in_vmem, slab)]
     specs = [SCALARS] + [ON_CHIP] * len(slab)
-    if halves:
-        out_shape = [
-            pltpu.VMEM((groups // 2, size, width), dtype)
-            for dtype in (jnp.bfloat16, jnp.float32)
-        ]
-    else:
-        out_shape = [pltpu.VMEM((groups, size, width), jnp.float32)]
-    scratch = [pltpu.VMEM((rows + size, width), slab[0].dtype)]
     if fetched:
         operands += [in_vmem(held), in_vmem(total)]
         specs += [ON_CHIP] * 2
-    else:
-        scratch += [pltpu.VMEM(shape, tiles.dtype), pltpu.SemaphoreType.DMA((1,))]
-    if ahead or not fetched:
+    if ahead or parts or not fetched:
         operands.append(in_hbm(tiles))
         specs.append(OFF_CHIP)
-    if ahead:
-        out_shape += [pltpu.VMEM(shape, tiles.dtype)] * len(ahead)
-        scratch.append(pltpu.SemaphoreType.DMA((len(ahead),)))
+    panels = pltpu.VMEM((rows + size, width), slab[0].dtype)
+    count = groups // 2 if halved else groups
+    out_shape = [pltpu.VMEM((count, size, width), jnp.float32)] * (groups // count)
+    out_shape += [pltpu.VMEM(shape, tiles.dtype)] * len(ahead)
+    for _, _, runs in parts:
+        run = (groups // 2 // runs, *shape[1:])
+        out_shape += [pltpu.VMEM(run, tiles.dtype)] * runs
+    later = len(ahead) + sum(runs for _, _, runs in parts)
+    scratch = [panels, pltpu.SemaphoreType.DMA((1 + later,))]
+    if not fetched:
+        scratch.append(pltpu.VMEM(shape, tiles.dtype))
     outs = pl.pallas_call(
         functools.partial(
-            product_kernel, step, fetched, tuple(ahead), halves, len(slab), spans
+            product_kernel, step, fetched, ahead, parts, halved, len(slab), spans
         ),
         out_shape=out_shape,
         in_specs=specs,
@@ -236,6 +280,58 @@
         cost_estimate=COST,
         name="product",
     )(*operands)
+    return outs if len(outs) > 1 else outs[0]
+
+
+def half_kernel(half, pieces, works, spans, *refs):
+    refs = list(refs)
+    tables = [refs.pop(0) for _ in works]
+    slab = [refs.pop(0) for _ in range(pieces or 1)]
+    tiles = [[refs.pop(0) for _ in range(count)] for _, count in works]
+    total, out = refs.pop(0), refs.pop(0)
+    groups, size, _ = out.shape
+    panels = slab[0]
+    if pieces:
+        panels = refs.pop(0)
+        place_slab(slab, panels, size)
+    start = halves(2 * groups)[half]
+    for g in range(groups):
+        lhs, rhs = [], []
+        for table, (step, count), runs in zip(tables, works, tiles):
+            slots, run = runs[0].shape[1], groups // count
+            first = (offset_of(step, spans) * (2 * groups) + start + g) * slots
+            more = terms(panels, table, first, slots, runs[g // run], g % run)
+            lhs, rhs = lhs + more[0], rhs + more[1]
+        out[g] = (total[g] + multiplied(lhs, rhs)).astype(out.dtype)
+
+
+def half_product(half, slab, works, total, spans, dtype=jnp.float32, placed=None):
+    _, size, width = total.shape
+    rows = sum(piece.shape[0] for piece in slab) + (0 if placed else size)
+    tables = [in_smem(table) for _, table, _ in works]
+    vmem = [*slab, *(runs for _, _, tiles in works for runs in tiles), total]
+    out_shape = [pltpu.VMEM(total.shape, dtype)]
+    panels, scratch = pltpu.VMEM((rows, width), slab[0].dtype), []
+    if placed is None:
+        scratch.append(panels)
+    elif not placed:
+        out_shape.append(panels)
+    outs = pl.pallas_call(
+        functools.partial(
+            half_kernel,
+            half,
+            0 if placed else len(slab),
+            [(step, len(tiles)) for step, _, tiles in works],
+            spans,
+        ),
+        out_shape=out_shape,
+        in_specs=[SCALARS] * len(tables) + [ON_CHIP] * len(vmem),
+        out_specs=[ON_CHIP] * len(out_shape),
+        scratch_shapes=scratch,
+        compiler_params=PARAMS,
+        cost_estimate=COST,
+        name="half_product",
+    )(*tables, *map(in_vmem, vmem))
     return outs if len(outs) > 1 else outs[0]
 
 
@@ -307,27 +403,54 @@
     count = jnp.broadcast_to(node_count[None], (8, node_feats.shape[1]))
     own = split(node_feats, count)
     near = [along_ring(piece) for piece in own]
-    total, near_tiles, near_other_tiles = product(
-        OWN, columns, own, tile_vals, ahead=(NEAR, NEAR_OTHER)
-    )
+    table = table_of(columns)
+    total, near_tiles, near_other_tiles, *gifts = product(
+        OWN,
+        table,
+        own,
+        tile_vals,
+        ahead=(NEAR, NEAR_OTHER),
+        parts=((FAR_OTHER, GIVEN, GIFTS),),
+    )
+    gifts = [between_cores(gift) for gift in gifts]
+    other_columns = between_cores(columns)
     first, (total, near_tiles, near_other_tiles) = after(
         near[0], (total, near_tiles, near_other_tiles)
     )
     near = [first, near[1]]
-    far = [along_ring(piece) for piece in near]
+    far = [further_along(piece) for piece in near]
     near_other = [between_cores(piece) for piece in thirds(near, size)]
-    total, far_tiles, far_other_tiles = product(
-        NEAR, columns, near, tile_vals, near_tiles, total, ahead=(FAR, FAR_OTHER)
-    )
-    total = product(NEAR_OTHER, columns, near_other, tile_vals, near_other_tiles, total)
-    first, total = after(far[0], total)
+    near_tiles, (gifts, other_columns) = after(near_tiles, (gifts, other_columns))
+    total, far_given_tiles, far_kept_tiles, far_other_tiles = product(
+        NEAR,
+        table,
+        near,
+        tile_vals,
+        near_tiles,
+        total,
+        parts=((FAR, GIVEN, 1), (FAR, KEPT, 1), (FAR_OTHER, KEPT, 1)),
+    )
+    total, other_table = after(total, table_of(other_columns))
+    totals = product(
+        NEAR_OTHER, table, near_other, tile_vals, near_other_tiles, total, halved=True
+    )
+    first, totals = after(far[0], totals)
     far = [first, far[1]]
     far_other = [between_cores(piece) for piece in far]
-    total = product(FAR, columns, far, tile_vals, far_tiles, total)
-    given, kept = product(
-        FAR_OTHER, columns, far_other, tile_vals, far_other_tiles, total, halves=True
+    given, far_panels = half_product(
+        GIVEN,
+        far,
+        [(FAR, table, [far_given_tiles])],
+        totals[0],
+        spans,
+        jnp.bfloat16,
+        placed=False,
     )
     got = between_cores(given)
+    works = [(FAR, table, [far_kept_tiles]), (FAR, other_table, gifts)]
+    kept = half_product(KEPT, [far_panels], works, totals[1], spans, placed=True)
+    works = [(FAR_OTHER, table, [far_other_tiles])]
+    kept = half_product(KEPT, far_other, works, kept, spans)
     mine = add(kept, got)
     theirs = between_feats(mine)
     out = finish(count, mine, weight_own, bias_own)

time: 52.7 us -> 49.2 us (0.934)
  starting transfers between devices: 29.4 us -> 21.6 us
  waiting for transfers between devices: 6.71 us -> 12.7 us
  Pallas kernels: 15.3 us -> 13.6 us
    ppermute x4 -> x2, starting transfers between devices: 21.9 us -> 10.3 us  [along_ring(): lax.ppermute(value, AXES, permutation(lambda t, r, f: (t + 1 - 2 * r, r,...]
    ppermute x0 -> x2, starting transfers between devices: none -> 6.25 us  [further_along(): lax.ppermute(value, AXES, permutation(lambda t, r, f: (t + 1 - 2 * r, 1 -...]
    ppermute x0 -> x2, waiting for transfers between devices: none -> 3.97 us  [further_along(): lax.ppermute(value, AXES, permutation(lambda t, r, f: (t + 1 - 2 * r, 1 -...]
    ppermute x6 -> x9, starting transfers between devices: 4.77 us -> 2.3 us  [between_cores(): return lax.ppermute(value, AXES, permutation(lambda t, r, f: (t, 1 - r, f)))]
    ppermute x4 -> x2, waiting for transfers between devices: 0.01 us -> 2 us  [along_ring(): lax.ppermute(value, AXES, permutation(lambda t, r, f: (t + 1 - 2 * r, r,...]
    pallas_call x5 -> x8, Pallas kernels: 11 us -> 9.26 us  [the longest x3 6.43 us: product(): pl.pallas_call(functools.partial(product_kernel, step, fetched, ahead, pa...]
    ppermute x6 -> x9, waiting for transfers between devices: 1.34 us -> 1.19 us  [between_cores(): return lax.ppermute(value, AXES, permutation(lambda t, r, f: (t, 1 - r, f)))]
  transfers between devices with their start and end apart: 11 -> 14, of which waited for: 3 -> 5; matrix products, arithmetic and copies ran while one was open for 1% -> 1% of each run, Pallas kernels for 23% -> 23%
where the time goes in v4:
time: 49.2 us; the launch traced here: 49.1 us
  starting transfers between devices  21.6 us (44%)
  Pallas kernels  13.6 us (28%)
  waiting for transfers between devices  12.7 us (26%)
  between operations  0.83 us (2%)
    ppermute x2, starting transfers between devices, along_ring(): lax.ppermute(value, AXES, permutation(lambda t, r, f: (t + 1 - 2 * r, r,...  10.3 us
    pallas_call x3, Pallas kernels, product(): pl.pallas_call(functools.partial(product_kernel, step, fetched, ahead, pa...  6.43 us
    ppermute x2, starting transfers between devices, further_along(): lax.ppermute(value, AXES, permutation(lambda t, r, f: (t + 1 - 2 * r, 1 -...  6.25 us
    ppermute x1, waiting for transfers between devices, between_feats(): return lax.ppermute(value, AXES, permutation(lambda t, r, f: (t, r, 1 - f)))  5.51 us
    ppermute x2, waiting for transfers between devices, further_along(): lax.ppermute(value, AXES, permutation(lambda t, r, f: (t + 1 - 2 * r, 1 -...  3.97 us
    ppermute x1, starting transfers between devices, between_feats(): return lax.ppermute(value, AXES, permutation(lambda t, r, f: (t, r, 1 - f)))  2.75 us
    ppermute x9, starting transfers between devices, between_cores(): return lax.ppermute(value, AXES, permutation(lambda t, r, f: (t, 1 - r, f)))  2.3 us
    ppermute x2, waiting for transfers between devices, along_ring(): lax.ppermute(value, AXES, permutation(lambda t, r, f: (t + 1 - 2 * r, r,...  2 us
  transfers between devices with their start and end apart: 14, of which 5 were waited for; matrix products, arithmetic and copies ran while one was open for 1% of the time, Pallas kernels for 23%

profile of v4, /device:TPU:1, one launch (start us, length us, event | category | flops | bytes accessed | tf_op | source)
XLA Modules:
  0.0 49.1 jit_solution(10312762971710744034)
XLA Ops:
  0.0 1.1 %head_of_slab.1.refs_0_ = bf16[2048,128]{1,0:T(8,128)(2,1)S(1)} custom-call(bf16[4096,128]{1,0:T(8,128)(2,1)} %feats.3), custom_call_target="tpu_custom_call" | custom-call | tf_op jit(solution)/shard_map/head_of_slab/pallas_call | solution.py:98
  1.1 9.7 %collective-permute-start = (bf16[2048,128]{1,0:T(8,128)(2,1)S(1)}, bf16[2048,128]{1,0:T(8,128)(2,1)S(1)}, u32[]{:S(2)}, u32[]{:S(2)}) collective-permute-start(bf16[2048,128]{1,0:T(8,128)(2,1)S(1)} %head_of_slab.1.refs_0_), channel_id=1, source_target_pairs={{0,4},{1,5},{2,254},{3,255},{4,8},{5,9},{6,2},{7,3},{8,12},{9,13},... | collective-permute-start | bytes 1572872 | tf_op jit(solution)/shard_map/ppermute | solution.py:31
  11.5 1.2 %tail_of_slab.1.refs_1_ = bf16[2048,128]{1,0:T(8,128)(2,1)S(1)} custom-call(s32[8,128]{1,0:T(8,128)S(1)} %broadcast_in_dim.17.count, bf16[4096,128]{1,0:T(8,128)(2,1)} %feats.3), custom_call_target="tpu_custom_call" | custom-call | tf_op jit(solution)/shard_map/tail_of_slab/pallas_call | solution.py:105
  12.7 0.6 %collective-permute-start.2 = (bf16[2048,128]{1,0:T(8,128)(2,1)S(1)}, bf16[2048,128]{1,0:T(8,128)(2,1)S(1)}, u32[]{:S(2)}, u32[]{:S(2)}) collective-permute-start(bf16[2048,128]{1,0:T(8,128)(2,1)S(1)} %tail_of_slab.1.refs_1_), channel_id=1, source_target_pairs={{0,4},{1,5},{2,254},{3,255},{4,8},{5,9},{6,2},{7,3},{8,12},{9,13},... | collective-permute-start | bytes 1572872 | tf_op jit(solution)/shard_map/ppermute | solution.py:31
  13.6 0.6 %table.2.refs_0_ = s32[320]{0:T(512)S(4)} custom-call(s32[320]{0:T(512)S(1)} %reshape.12.columns), custom_call_target="tpu_custom_call" | custom-call | tf_op jit(solution)/shard_map/table/pallas_call | solution.py:166
  14.2 3.1 %product.3 = (f32[16,128,128]{2,1,0:T(8,128)S(1)}, bf16[16,4,128,128]{3,2,1,0:T(8,128)(2,1)S(1)}, bf16[16,4,128,128]{3,2,1,0:T(8,128)(2,1)S(1)}, bf16[4,4,128,12...) custom-call(s32[320]{0:T(512)S(4)} %table.2.refs_0_, bf16[2048,128]{1,0:T(8,128)(2,1)S(1)} %head_of_slab.1.refs_0_, ...), custom_call_target="tpu_custom_call" | custom-call | tf_op jit(solution)/shard_map/product/pallas_call | solution.py:271
  17.4 0.5 %collective-permute-start.7 = (bf16[4,4,128,128]{3,2,1,0:T(8,128)(2,1)S(1)}, bf16[4,4,128,128]{3,2,1,0:T(8,128)(2,1)S(1)}, u32[]{:S(2)}, u32[]{:S(2)}) collective-permute-start(bf16[4,4,128,128]{3,2,1,0:T(8,128)(2,1)S(1)} %get-tuple-element.44), channel_id=1, source_target_pairs={{0,2},{1,3},{2,0},{3,1},{4,6},{5,7},{6,4},{7,5},{8,10},{9,11},{10,... | collective-permute-start | bytes 1572872 | tf_op jit(solution)/shard_map/ppermute | solution.py:39
  17.9 2.6 %collective-permute-start.1 = (bf16[2048,128]{1,0:T(8,128)(2,1)S(1)}, bf16[2048,128]{1,0:T(8,128)(2,1)S(1)}, u32[]{:S(2)}, u32[]{:S(2)}) collective-permute-start(bf16[2048,128]{1,0:T(8,128)(2,1)S(1)} %collective-permute-done.head.refs_0_), channel_id=1, source_target_pairs={{0,6},{1,7},{2,252},{3,253},{4,10},{5,11},{6,0},{7,1},{8,14},{9,15... | collective-permute-start | bytes 1572872 | tf_op jit(solution)/shard_map/ppermute | solution.py:35
  20.5 2.0 %collective-permute-done.2.tail.refs_1_ = bf16[2048,128]{1,0:T(8,128)(2,1)S(1)} collective-permute-done((bf16[2048,128]{1,0:T(8,128)(2,1)S(1)}, bf16[2048,128]{1,0:T(8,128)(2,1)S(1)}, u32[]{:S(2)}, u32[]{:S(2)}) %collective-permute-start.2) | collective-permute-done | bytes 524320 | tf_op jit(solution)/shard_map/ppermute | solution.py:31
  22.5 3.6 %collective-permute-start.10 = (bf16[2048,128]{1,0:T(8,128)(2,1)S(1)}, bf16[2048,128]{1,0:T(8,128)(2,1)S(1)}, u32[]{:S(2)}, u32[]{:S(2)}) collective-permute-start(bf16[2048,128]{1,0:T(8,128)(2,1)S(1)} %collective-permute-done.2.tail.refs_1_), channel_id=1, source_target_pairs={{0,6},{1,7},{2,252},{3,253},{4,10},{5,11},{6,0},{7,1},{8,14},{9,15... | collective-permute-start | bytes 1572872 | tf_op jit(solution)/shard_map/ppermute | solution.py:35
  26.2 1.1 %collective-permute-done.8.columns = s32[320]{0:T(512)S(1)} collective-permute-done((s32[320]{0:T(512)S(1)}, s32[320]{0:T(512)S(1)}, u32[]{:S(2)}, u32[]{:S(2)}) %collective-permute-start.8) | collective-permute-done | bytes 1312 | tf_op jit(solution)/shard_map/ppermute | solution.py:39
  28.0 0.6 %table.3.refs_1_ = s32[320]{0:T(512)S(4)} custom-call(s32[320]{0:T(512)S(1)} %collective-permute-done.8.columns), custom_call_target="tpu_custom_call" | custom-call | tf_op jit(solution)/shard_map/table/pallas_call | solution.py:166
  28.6 2.5 %product.4 = (f32[16,128,128]{2,1,0:T(8,128)S(1)}, bf16[8,4,128,128]{3,2,1,0:T(8,128)(2,1)S(1)}, bf16[8,4,128,128]{3,2,1,0:T(8,128)(2,1)S(1)}, bf16[8,4,128,128]{3,2,1,0:T(8,128)(2,1)S(1)}) custom-call(s32[320]{0:T(512)S(4)} %table.2.refs_0_, bf16[2048,128]{1,0:T(8,128)(2,1)S(1)} %collective-permute-done.head.refs_0_, ...), custom_call_target="tpu_custom_call" | custom-call | tf_op jit(solution)/shard_map/product/pallas_call | solution.py:271
  31.2 0.8 %product.5 = (f32[8,128,128]{2,1,0:T(8,128)S(1)}, f32[8,128,128]{2,1,0:T(8,128)S(1)}) custom-call(s32[320]{0:T(512)S(4)} %table.2.refs_0_, bf16[1536,128]{1,0:T(8,128)(2,1)S(1)} %collective-permute-done.3.refs_0_, bf16[1280,128]{1,0:T(8,128)(2,1)S(1)} %collective-permute-done.4.refs_1_, bf16[1280,128]{1,0:T(8,128)(2,1)S(1)} %collective-permute-done.5.refs_2_, ...), custom_call_target="tpu_custom_call" | custom-call | tf_op jit(solution)/shard_map/product/pallas_call | solution.py:271
  32.0 0.4 collective-permute-start.9
  32.4 4.0 %collective-permute-done.10.refs_2_ = bf16[2048,128]{1,0:T(8,128)(2,1)S(1)} collective-permute-done((bf16[2048,128]{1,0:T(8,128)(2,1)S(1)}, bf16[2048,128]{1,0:T(8,128)(2,1)S(1)}, u32[]{:S(2)}, u32[]{:S(2)}) %collective-permute-start.10) | collective-permute-done | bytes 524320 | tf_op jit(solution)/shard_map/ppermute | solution.py:35
  36.3 0.5 %half_product.3 = (bf16[8,128,128]{2,1,0:T(8,128)(2,1)S(1)}, bf16[4224,128]{1,0:T(8,128)(2,1)S(1)}) custom-call(s32[320]{0:T(512)S(4)} %table.2.refs_0_, bf16[2048,128]{1,0:T(8,128)(2,1)S(1)} %collective-permute-done.1.refs_1_, bf16[2048,128]{1,0:T(8,128)(2,1)S(1)} %collective-permute-done.10.refs_2_, ...), custom_call_target="tpu_custom_call" | custom-call | tf_op jit(solution)/shard_map/half_product/pallas_call | solution.py:319
  36.8 0.6 %collective-permute-start.12 = (bf16[8,128,128]{2,1,0:T(8,128)(2,1)S(1)}, bf16[8,128,128]{2,1,0:T(8,128)(2,1)S(1)}, u32[]{:S(2)}, u32[]{:S(2)}) collective-permute-start(bf16[8,128,128]{2,1,0:T(8,128)(2,1)S(1)} %get-tuple-element.62), channel_id=1, source_target_pairs={{0,2},{1,3},{2,0},{3,1},{4,6},{5,7},{6,4},{7,5},{8,10},{9,11},{10,... | collective-permute-start | bytes 786440 | tf_op jit(solution)/shard_map/ppermute | solution.py:39
  37.4 0.7 %half_product.4.refs_4_ = f32[8,128,128]{2,1,0:T(8,128)S(1)} custom-call(s32[320]{0:T(512)S(4)} %table.2.refs_0_, s32[320]{0:T(512)S(4)} %table.3.refs_1_, bf16[4224,128]{1,0:T(8,128)(2,1)S(1)} %get-tuple-element.57.refs_2_, bf16[8,4,128,128]{3,2,1,0:T(8,128)(2,1)S(1)} %get-tuple-element.58.refs_3_, ...), custom_call_target="tpu_custom_call" | custom-call | tf_op jit(solution)/shard_map/half_product/pallas_call | solution.py:319
  38.3 0.5 %half_product.5.kept = f32[8,128,128]{2,1,0:T(8,128)S(1)} custom-call(s32[320]{0:T(512)S(4)} %table.2.refs_0_, bf16[2048,128]{1,0:T(8,128)(2,1)S(1)} %collective-permute-done.9.refs_1_, bf16[2048,128]{1,0:T(8,128)(2,1)S(1)} %collective-permute-done.11.refs_2_, bf16[8,4,128,128]{3,2,1,0:T(8,128)(2,1)S(1)} %get-tuple-element.53.refs_3_, ...), custom_call_target="tpu_custom_call" | custom-call | tf_op jit(solution)/shard_map/half_product/pallas_call | solution.py:319
  38.8 2.8 %collective-permute-start.13 = (bf16[8,128,128]{2,1,0:T(8,128)(2,1)S(1)}, bf16[8,128,128]{2,1,0:T(8,128)(2,1)S(1)}, u32[]{:S(2)}, u32[]{:S(2)}) collective-permute-start(bf16[8,128,128]{2,1,0:T(8,128)(2,1)S(1)} %add_halves.1.agg), channel_id=1, source_target_pairs={{0,1},{1,0},{2,3},{3,2},{4,5},{5,4},{6,7},{7,6},{8,9},{9,8},{10,11... | collective-permute-start | bytes 786440 | tf_op jit(solution)/shard_map/ppermute | solution.py:43
  41.7 0.9 %finish.2.refs_0_ = bf16[8,2,128,128]{3,2,1,0:T(8,128)(2,1)} custom-call(s32[8,128]{1,0:T(8,128)S(1)} %broadcast_in_dim.17.count, bf16[8,128,128]{2,1,0:T(8,128)(2,1)S(1)} %add_halves.1.agg, bf16[128,128]{1,0:T(8,128)(2,1)S(1)} %constant_dynamic-slice_fusion.weight, bf16[1,128]{1,0:T(2,128)(2,1)S(1)} %dynamic-slice_bitcast_fusion.bias), custom_call_target="tpu_custom_call" | custom-call | tf_op jit(solution)/shard_map/finish/pallas_call | solution.py:374
  42.6 5.5 %collective-permute-done.13.agg = bf16[8,128,128]{2,1,0:T(8,128)(2,1)S(1)} collective-permute-done((bf16[8,128,128]{2,1,0:T(8,128)(2,1)S(1)}, bf16[8,128,128]{2,1,0:T(8,128)(2,1)S(1)}, u32[]{:S(2)}, u32[]{:S(2)}) %collective-permute-start.13) | collective-permute-done | bytes 262176 | tf_op jit(solution)/shard_map/ppermute | solution.py:43
  48.1 0.9 %finish.3 = bf16[8,2,128,128]{3,2,1,0:T(8,128)(2,1)} custom-call(s32[8,128]{1,0:T(8,128)S(1)} %broadcast_in_dim.17.count, bf16[8,128,128]{2,1,0:T(8,128)(2,1)S(1)} %collective-permute-done.13.agg, bf16[128,128]{1,0:T(8,128)(2,1)S(1)} %constant_dynamic-slice_fusion.weight, ...), custom_call_target="tpu_custom_call", output_to_operand_aliasing={{}: (4, {})} | custom-call | tf_op jit(solution)/shard_map/finish/pallas_call | solution.py:374
  (34 shorter events, 1.4 us)
Async XLA Ops:
  0.0 41.7 %copy-start = (bf16[128,256]{1,0:T(8,128)(2,1)S(1)}, bf16[128,256]{1,0:T(8,128)(2,1)}, u32[]{:S(2)}) copy-start(bf16[128,256]{1,0:T(8,128)(2,1)} %param.12) | copy-start | bytes 196612
  0.0 13.3 %copy-start.2 = (s32[16,1,5]{0,1,2:T(1,128)S(1)}, s32[16,1,5]{0,1,2:T(1,128)}, u32[]{:S(2)}) copy-start(s32[16,1,5]{0,1,2:T(1,128)} %param.10) | copy-start | bytes 964
  0.0 13.3 %copy-start.1 = (s32[16,1,5,4]{0,3,2,1:T(4,128)S(1)}, s32[16,1,5,4]{0,3,2,1:T(4,128)}, u32[]{:S(2)}) copy-start(s32[16,1,5,4]{0,3,2,1:T(4,128)} %param.9) | copy-start | bytes 3844
  1.1 16.8 %collective-permute-start = (bf16[2048,128]{1,0:T(8,128)(2,1)S(1)}, bf16[2048,128]{1,0:T(8,128)(2,1)S(1)}, u32[]{:S(2)}, u32[]{:S(2)}) collective-permute-start(bf16[2048,128]{1,0:T(8,128)(2,1)S(1)} %head_of_slab.1.refs_0_), channel_id=1, source_target_pairs={{0,4},{1,5},{2,254},{3,255},{4,8},{5,9},{6,2},{7,3},{8,12},{9,13},... | collective-permute-start | bytes 1572872 | tf_op jit(solution)/shard_map/ppermute | solution.py:31
  12.7 9.9 %collective-permute-start.2 = (bf16[2048,128]{1,0:T(8,128)(2,1)S(1)}, bf16[2048,128]{1,0:T(8,128)(2,1)S(1)}, u32[]{:S(2)}, u32[]{:S(2)}) collective-permute-start(bf16[2048,128]{1,0:T(8,128)(2,1)S(1)} %tail_of_slab.1.refs_1_), channel_id=1, source_target_pairs={{0,4},{1,5},{2,254},{3,255},{4,8},{5,9},{6,2},{7,3},{8,12},{9,13},... | collective-permute-start | bytes 1572872 | tf_op jit(solution)/shard_map/ppermute | solution.py:31
  17.3 10.2 %collective-permute-start.6 = (bf16[4,4,128,128]{3,2,1,0:T(8,128)(2,1)S(1)}, bf16[4,4,128,128]{3,2,1,0:T(8,128)(2,1)S(1)}, u32[]{:S(2)}, u32[]{:S(2)}) collective-permute-start(bf16[4,4,128,128]{3,2,1,0:T(8,128)(2,1)S(1)} %get-tuple-element.43), channel_id=1, source_target_pairs={{0,2},{1,3},{2,0},{3,1},{4,6},{5,7},{6,4},{7,5},{8,10},{9,11},{10,... | collective-permute-start | bytes 1572872 | tf_op jit(solution)/shard_map/ppermute | solution.py:39
  17.4 10.4 %collective-permute-start.7 = (bf16[4,4,128,128]{3,2,1,0:T(8,128)(2,1)S(1)}, bf16[4,4,128,128]{3,2,1,0:T(8,128)(2,1)S(1)}, u32[]{:S(2)}, u32[]{:S(2)}) collective-permute-start(bf16[4,4,128,128]{3,2,1,0:T(8,128)(2,1)S(1)} %get-tuple-element.44), channel_id=1, source_target_pairs={{0,2},{1,3},{2,0},{3,1},{4,6},{5,7},{6,4},{7,5},{8,10},{9,11},{10,... | collective-permute-start | bytes 1572872 | tf_op jit(solution)/shard_map/ppermute | solution.py:39
  17.9 14.0 %collective-permute-start.1 = (bf16[2048,128]{1,0:T(8,128)(2,1)S(1)}, bf16[2048,128]{1,0:T(8,128)(2,1)S(1)}, u32[]{:S(2)}, u32[]{:S(2)}) collective-permute-start(bf16[2048,128]{1,0:T(8,128)(2,1)S(1)} %collective-permute-done.head.refs_0_), channel_id=1, source_target_pairs={{0,6},{1,7},{2,252},{3,253},{4,10},{5,11},{6,0},{7,1},{8,14},{9,15... | collective-permute-start | bytes 1572872 | tf_op jit(solution)/shard_map/ppermute | solution.py:35
  22.5 13.8 %collective-permute-start.10 = (bf16[2048,128]{1,0:T(8,128)(2,1)S(1)}, bf16[2048,128]{1,0:T(8,128)(2,1)S(1)}, u32[]{:S(2)}, u32[]{:S(2)}) collective-permute-start(bf16[2048,128]{1,0:T(8,128)(2,1)S(1)} %collective-permute-done.2.tail.refs_1_), channel_id=1, source_target_pairs={{0,6},{1,7},{2,252},{3,253},{4,10},{5,11},{6,0},{7,1},{8,14},{9,15... | collective-permute-start | bytes 1572872 | tf_op jit(solution)/shard_map/ppermute | solution.py:35
  26.2 1.2 %collective-permute-start.8 = (s32[320]{0:T(512)S(1)}, s32[320]{0:T(512)S(1)}, u32[]{:S(2)}, u32[]{:S(2)}) collective-permute-start(s32[320]{0:T(512)S(1)} %reshape.12.columns), channel_id=1, source_target_pairs={{0,2},{1,3},{2,0},{3,1},{4,6},{5,7},{6,4},{7,5},{8,10},{9,11},{10,... | collective-permute-start | bytes 3848 | tf_op jit(solution)/shard_map/ppermute | solution.py:39
  27.3 3.8 %collective-permute-start.3 = (bf16[1536,128]{1,0:T(8,128)(2,1)S(1)}, bf16[1536,128]{1,0:T(8,128)(2,1)S(1)}, u32[]{:S(2)}, u32[]{:S(2)}) collective-permute-start(bf16[1536,128]{1,0:T(8,128)(2,1)S(1)} %get-tuple-element.38), channel_id=1, source_target_pairs={{0,2},{1,3},{2,0},{3,1},{4,6},{5,7},{6,4},{7,5},{8,10},{9,11},{10,... | collective-permute-start | bytes 1179656 | tf_op jit(solution)/shard_map/ppermute | solution.py:39
  27.5 3.6 %collective-permute-start.4 = (bf16[1280,128]{1,0:T(8,128)(2,1)S(1)}, bf16[1280,128]{1,0:T(8,128)(2,1)S(1)}, u32[]{:S(2)}, u32[]{:S(2)}) collective-permute-start(bf16[1280,128]{1,0:T(8,128)(2,1)S(1)} %get-tuple-element.39), channel_id=1, source_target_pairs={{0,2},{1,3},{2,0},{3,1},{4,6},{5,7},{6,4},{7,5},{8,10},{9,11},{10,... | collective-permute-start | bytes 983048 | tf_op jit(solution)/shard_map/ppermute | solution.py:39
  27.8 3.3 %collective-permute-start.5 = (bf16[1280,128]{1,0:T(8,128)(2,1)S(1)}, bf16[1280,128]{1,0:T(8,128)(2,1)S(1)}, u32[]{:S(2)}, u32[]{:S(2)}) collective-permute-start(bf16[1280,128]{1,0:T(8,128)(2,1)S(1)} %get-tuple-element.40), channel_id=1, source_target_pairs={{0,2},{1,3},{2,0},{3,1},{4,6},{5,7},{6,4},{7,5},{8,10},{9,11},{10,... | collective-permute-start | bytes 983048 | tf_op jit(solution)/shard_map/ppermute | solution.py:39
  32.0 6.2 %collective-permute-start.9 = (bf16[2048,128]{1,0:T(8,128)(2,1)S(1)}, bf16[2048,128]{1,0:T(8,128)(2,1)S(1)}, u32[]{:S(2)}, u32[]{:S(2)}) collective-permute-start(bf16[2048,128]{1,0:T(8,128)(2,1)S(1)} %collective-permute-done.1.refs_1_), channel_id=1, source_target_pairs={{0,2},{1,3},{2,0},{3,1},{4,6},{5,7},{6,4},{7,5},{8,10},{9,11},{10,... | collective-permute-start | bytes 1572872 | tf_op jit(solution)/shard_map/ppermute | solution.py:39
  36.3 1.9 %collective-permute-start.11 = (bf16[2048,128]{1,0:T(8,128)(2,1)S(1)}, bf16[2048,128]{1,0:T(8,128)(2,1)S(1)}, u32[]{:S(2)}, u32[]{:S(2)}) collective-permute-start(bf16[2048,128]{1,0:T(8,128)(2,1)S(1)} %collective-permute-done.10.refs_2_), channel_id=1, source_target_pairs={{0,2},{1,3},{2,0},{3,1},{4,6},{5,7},{6,4},{7,5},{8,10},{9,11},{10,... | collective-permute-start | bytes 1572872 | tf_op jit(solution)/shard_map/ppermute | solution.py:39
  36.8 1.9 %collective-permute-start.12 = (bf16[8,128,128]{2,1,0:T(8,128)(2,1)S(1)}, bf16[8,128,128]{2,1,0:T(8,128)(2,1)S(1)}, u32[]{:S(2)}, u32[]{:S(2)}) collective-permute-start(bf16[8,128,128]{2,1,0:T(8,128)(2,1)S(1)} %get-tuple-element.62), channel_id=1, source_target_pairs={{0,2},{1,3},{2,0},{3,1},{4,6},{5,7},{6,4},{7,5},{8,10},{9,11},{10,... | collective-permute-start | bytes 786440 | tf_op jit(solution)/shard_map/ppermute | solution.py:39
  38.3 3.3 %copy-start.3 = (bf16[256]{0:T(256)(128)(2,1)S(1)}, bf16[256]{0:T(256)(128)(2,1)}, u32[]{:S(2)}) copy-start(bf16[256]{0:T(256)(128)(2,1)} %param.13) | copy-start | bytes 1540
  38.8 9.3 %collective-permute-start.13 = (bf16[8,128,128]{2,1,0:T(8,128)(2,1)S(1)}, bf16[8,128,128]{2,1,0:T(8,128)(2,1)S(1)}, u32[]{:S(2)}, u32[]{:S(2)}) collective-permute-start(bf16[8,128,128]{2,1,0:T(8,128)(2,1)S(1)} %add_halves.1.agg), channel_id=1, source_target_pairs={{0,1},{1,0},{2,3},{3,2},{4,5},{5,4},{6,7},{7,6},{8,9},{9,8},{10,11... | collective-permute-start | bytes 786440 | tf_op jit(solution)/shard_map/ppermute | solution.py:43

commit v5 on v4

--- a/solution.py
+++ b/solution.py
@@ -69,10 +69,17 @@
 PARAMS = pltpu.CompilerParams(vmem_limit_bytes=VMEM_LIMIT)
 
 
-def head_kernel(feats, out, sem):
-    copy = pltpu.make_async_copy(feats.at[pl.ds(0, out.shape[0])], out, sem)
-    copy.start()
-    copy.wait()
+def head_kernel(feats, out, sems):
+    runs = sems.shape[0]
+    rows = out.shape[0] // runs
+    copies = []
+    for i in range(runs):
+        run = pl.ds(i * rows, rows)
+        copies.append(pltpu.make_async_copy(feats.at[run], out.at[run], sems.at[i]))
+    for copy in copies:
+        copy.start()
+    for copy in copies:
+        copy.wait()
 
 
 def tail_kernel(first, count, feats, out, held, sem):
@@ -98,7 +105,7 @@
     head = pl.pallas_call(
         head_kernel,
         in_specs=[OFF_CHIP],
-        scratch_shapes=[pltpu.SemaphoreType.DMA],
+        scratch_shapes=[pltpu.SemaphoreType.DMA((2,))],
         name="head_of_slab",
         **options,
     )(node_feats)
@@ -351,7 +358,8 @@
 
 
 def finish_kernel(other, count, agg, weight, bias, *refs):
-    out, held, sem = refs[-3:]
+    out, held, sems = refs[-3:]
+    copies = []
     groups, size, _ = agg.shape
     feat = lax.axis_index("feat")
     feat = 1 - feat if other else feat
@@ -362,9 +370,13 @@
         value = jnp.dot(agg[g], weight[...], preferred_element_type=jnp.float32)
         value = jnp.maximum(value + biased, 0.0)
         held[g] = jnp.where(row + 2 * g * size < live, value, 0.0).astype(out.dtype)
-    copy = pltpu.make_async_copy(held, out.at[:, feat], sem)
-    copy.start()
-    copy.wait()
+        if (g + 1) % (groups // 2) == 0:
+            run = pl.ds(g + 1 - groups // 2, groups // 2)
+            source, target = held.at[run], out.at[run, feat]
+            copies.append(pltpu.make_async_copy(source, target, sems.at[len(copies)]))
+            copies[-1].start()
+    for copy in copies:
+        copy.wait()
 
 
 def finish(count, agg, weight, bias, out=None):
@@ -378,7 +390,7 @@
         out_specs=OFF_CHIP,
         scratch_shapes=[
             pltpu.VMEM((groups, size, share), agg.dtype),
-            pltpu.SemaphoreType.DMA,
+            pltpu.SemaphoreType.DMA((2,)),
         ],
         input_output_aliases={4: 0} if before else {},
         compiler_params=PARAMS,
@@ -404,30 +416,29 @@
     own = split(node_feats, count)
     near = [along_ring(piece) for piece in own]
     table = table_of(columns)
-    total, near_tiles, near_other_tiles, *gifts = product(
+    total, near_tiles, *gifts = product(
         OWN,
         table,
         own,
         tile_vals,
-        ahead=(NEAR, NEAR_OTHER),
+        ahead=(NEAR,),
         parts=((FAR_OTHER, GIVEN, GIFTS),),
     )
     gifts = [between_cores(gift) for gift in gifts]
     other_columns = between_cores(columns)
-    first, (total, near_tiles, near_other_tiles) = after(
-        near[0], (total, near_tiles, near_other_tiles)
-    )
+    first, (total, near_tiles) = after(near[0], (total, near_tiles))
     near = [first, near[1]]
     far = [further_along(piece) for piece in near]
     near_other = [between_cores(piece) for piece in thirds(near, size)]
     near_tiles, (gifts, other_columns) = after(near_tiles, (gifts, other_columns))
-    total, far_given_tiles, far_kept_tiles, far_other_tiles = product(
+    total, near_other_tiles, far_given_tiles, far_kept_tiles, far_other_tiles = product(
         NEAR,
         table,
         near,
         tile_vals,
         near_tiles,
         total,
+        ahead=(NEAR_OTHER,),
         parts=((FAR, GIVEN, 1), (FAR, KEPT, 1), (FAR_OTHER, KEPT, 1)),
     )
     total, other_table = after(total, table_of(other_columns))

time: 49.2 us -> 48.6 us (0.988)
  waiting for transfers between devices: 12.7 us -> 11.5 us
  starting transfers between devices: 21.6 us -> 22.2 us
    ppermute x2, waiting for transfers between devices: 3.97 us -> 2.72 us  [further_along(): lax.ppermute(value, AXES, permutation(lambda t, r, f: (t + 1 - 2 * r, 1 -...]
    ppermute x2, starting transfers between devices: 6.25 us -> 6.86 us  [further_along(): lax.ppermute(value, AXES, permutation(lambda t, r, f: (t + 1 - 2 * r, 1 -...]
  transfers between devices with their start and end apart: 14 -> 14, of which waited for: 5 -> 5; matrix products, arithmetic and copies ran while one was open for 1% -> 1% of each run, Pallas kernels for 23% -> 24%
where the time goes in v5:
time: 48.6 us; the launch traced here: 48.4 us
  starting transfers between devices  22.2 us (46%)
  Pallas kernels  13.5 us (28%)
  waiting for transfers between devices  11.5 us (24%)
  between operations  0.83 us (2%)
    ppermute x2, starting transfers between devices, along_ring(): lax.ppermute(value, AXES, permutation(lambda t, r, f: (t + 1 - 2 * r, r,...  10.3 us
    ppermute x2, starting transfers between devices, further_along(): lax.ppermute(value, AXES, permutation(lambda t, r, f: (t + 1 - 2 * r, 1 -...  6.86 us
    pallas_call x3, Pallas kernels, product(): pl.pallas_call(functools.partial(product_kernel, step, fetched, ahead, pa...  6.46 us
    ppermute x1, waiting for transfers between devices, between_feats(): return lax.ppermute(value, AXES, permutation(lambda t, r, f: (t, r, 1 - f)))  5.6 us
    ppermute x2, waiting for transfers between devices, further_along(): lax.ppermute(value, AXES, permutation(lambda t, r, f: (t + 1 - 2 * r, 1 -...  2.72 us
    ppermute x1, starting transfers between devices, between_feats(): return lax.ppermute(value, AXES, permutation(lambda t, r, f: (t, r, 1 - f)))  2.71 us
    ppermute x9, starting transfers between devices, between_cores(): return lax.ppermute(value, AXES, permutation(lambda t, r, f: (t, 1 - r, f)))  2.3 us
    ppermute x2, waiting for transfers between devices, along_ring(): lax.ppermute(value, AXES, permutation(lambda t, r, f: (t + 1 - 2 * r, r,...  2 us
  transfers between devices with their start and end apart: 14, of which 5 were waited for; matrix products, arithmetic and copies ran while one was open for 1% of the time, Pallas kernels for 24%

profile of v5, /device:TPU:1, one launch (start us, length us, event | category | flops | bytes accessed | tf_op | source)
XLA Modules:
  0.0 48.4 jit_solution(1469838337565576413)
XLA Ops:
  0.0 1.1 %head_of_slab.1.refs_0_ = bf16[2048,128]{1,0:T(8,128)(2,1)S(1)} custom-call(bf16[4096,128]{1,0:T(8,128)(2,1)} %feats.3), custom_call_target="tpu_custom_call" | custom-call | tf_op jit(solution)/shard_map/head_of_slab/pallas_call | solution.py:105
  1.1 9.7 %collective-permute-start = (bf16[2048,128]{1,0:T(8,128)(2,1)S(1)}, bf16[2048,128]{1,0:T(8,128)(2,1)S(1)}, u32[]{:S(2)}, u32[]{:S(2)}) collective-permute-start(bf16[2048,128]{1,0:T(8,128)(2,1)S(1)} %head_of_slab.1.refs_0_), channel_id=1, source_target_pairs={{0,4},{1,5},{2,254},{3,255},{4,8},{5,9},{6,2},{7,3},{8,12},{9,13},... | collective-permute-start | bytes 1572872 | tf_op jit(solution)/shard_map/ppermute | solution.py:31
  11.5 1.2 %tail_of_slab.1.refs_1_ = bf16[2048,128]{1,0:T(8,128)(2,1)S(1)} custom-call(s32[8,128]{1,0:T(8,128)S(1)} %broadcast_in_dim.17.count, bf16[4096,128]{1,0:T(8,128)(2,1)} %feats.3), custom_call_target="tpu_custom_call" | custom-call | tf_op jit(solution)/shard_map/tail_of_slab/pallas_call | solution.py:112
  12.7 0.6 %collective-permute-start.2 = (bf16[2048,128]{1,0:T(8,128)(2,1)S(1)}, bf16[2048,128]{1,0:T(8,128)(2,1)S(1)}, u32[]{:S(2)}, u32[]{:S(2)}) collective-permute-start(bf16[2048,128]{1,0:T(8,128)(2,1)S(1)} %tail_of_slab.1.refs_1_), channel_id=1, source_target_pairs={{0,4},{1,5},{2,254},{3,255},{4,8},{5,9},{6,2},{7,3},{8,12},{9,13},... | collective-permute-start | bytes 1572872 | tf_op jit(solution)/shard_map/ppermute | solution.py:31
  13.6 0.6 %table.2.refs_0_ = s32[320]{0:T(512)S(4)} custom-call(s32[320]{0:T(512)S(1)} %reshape.12.columns), custom_call_target="tpu_custom_call" | custom-call | tf_op jit(solution)/shard_map/table/pallas_call | solution.py:173
  14.2 2.5 %product.3 = (f32[16,128,128]{2,1,0:T(8,128)S(1)}, bf16[16,4,128,128]{3,2,1,0:T(8,128)(2,1)S(1)}, bf16[4,4,128,128]{3,2,1,0:T(8,128)(2,1)S(1)}, bf16[4,4,128,128]{3,2,1,0:T(8,128)(2,1)S(1)}) custom-call(s32[320]{0:T(512)S(4)} %table.2.refs_0_, bf16[2048,128]{1,0:T(8,128)(2,1)S(1)} %head_of_slab.1.refs_0_, bf16[2048,128]{1,0:T(8,128)(2,1)S(1)} %tail_of_slab.1.refs_1_, ...), custom_call_target="tpu_custom_call" | custom-call | tf_op jit(solution)/shard_map/product/pallas_call | solution.py:278
  16.8 0.5 %collective-permute-start.7 = (bf16[4,4,128,128]{3,2,1,0:T(8,128)(2,1)S(1)}, bf16[4,4,128,128]{3,2,1,0:T(8,128)(2,1)S(1)}, u32[]{:S(2)}, u32[]{:S(2)}) collective-permute-start(bf16[4,4,128,128]{3,2,1,0:T(8,128)(2,1)S(1)} %get-tuple-element.41), channel_id=1, source_target_pairs={{0,2},{1,3},{2,0},{3,1},{4,6},{5,7},{6,4},{7,5},{8,10},{9,11},{10,... | collective-permute-start | bytes 1572872 | tf_op jit(solution)/shard_map/ppermute | solution.py:39
  17.3 3.2 %collective-permute-start.1 = (bf16[2048,128]{1,0:T(8,128)(2,1)S(1)}, bf16[2048,128]{1,0:T(8,128)(2,1)S(1)}, u32[]{:S(2)}, u32[]{:S(2)}) collective-permute-start(bf16[2048,128]{1,0:T(8,128)(2,1)S(1)} %collective-permute-done.head.refs_0_), channel_id=1, source_target_pairs={{0,6},{1,7},{2,252},{3,253},{4,10},{5,11},{6,0},{7,1},{8,14},{9,15... | collective-permute-start | bytes 1572872 | tf_op jit(solution)/shard_map/ppermute | solution.py:35
  20.5 2.0 %collective-permute-done.2.tail.refs_1_ = bf16[2048,128]{1,0:T(8,128)(2,1)S(1)} collective-permute-done((bf16[2048,128]{1,0:T(8,128)(2,1)S(1)}, bf16[2048,128]{1,0:T(8,128)(2,1)S(1)}, u32[]{:S(2)}, u32[]{:S(2)}) %collective-permute-start.2) | collective-permute-done | bytes 524320 | tf_op jit(solution)/shard_map/ppermute | solution.py:31
  22.5 3.6 %collective-permute-start.10 = (bf16[2048,128]{1,0:T(8,128)(2,1)S(1)}, bf16[2048,128]{1,0:T(8,128)(2,1)S(1)}, u32[]{:S(2)}, u32[]{:S(2)}) collective-permute-start(bf16[2048,128]{1,0:T(8,128)(2,1)S(1)} %collective-permute-done.2.tail.refs_1_), channel_id=1, source_target_pairs={{0,6},{1,7},{2,252},{3,253},{4,10},{5,11},{6,0},{7,1},{8,14},{9,15... | collective-permute-start | bytes 1572872 | tf_op jit(solution)/shard_map/ppermute | solution.py:35
  26.2 1.1 %collective-permute-done.8.columns = s32[320]{0:T(512)S(1)} collective-permute-done((s32[320]{0:T(512)S(1)}, s32[320]{0:T(512)S(1)}, u32[]{:S(2)}, u32[]{:S(2)}) %collective-permute-start.8) | collective-permute-done | bytes 1312 | tf_op jit(solution)/shard_map/ppermute | solution.py:39
  28.0 0.6 %table.3.refs_1_ = s32[320]{0:T(512)S(4)} custom-call(s32[320]{0:T(512)S(1)} %collective-permute-done.8.columns), custom_call_target="tpu_custom_call" | custom-call | tf_op jit(solution)/shard_map/table/pallas_call | solution.py:173
  28.6 3.2 %product.4 = (f32[16,128,128]{2,1,0:T(8,128)S(1)}, bf16[16,4,128,128]{3,2,1,0:T(8,128)(2,1)S(1)}, bf16[8,4,128,128]{3,2,1,0:T(8,128)(2,1)S(1)}, bf16[8,4,128,128...) custom-call(s32[320]{0:T(512)S(4)} %table.2.refs_0_, bf16[2048,128]{1,0:T(8,128)(2,1)S(1)} %collective-permute-done.head.refs_0_, ...), custom_call_target="tpu_custom_call" | custom-call | tf_op jit(solution)/shard_map/product/pallas_call | solution.py:278
  31.8 0.8 %product.5 = (f32[8,128,128]{2,1,0:T(8,128)S(1)}, f32[8,128,128]{2,1,0:T(8,128)S(1)}) custom-call(s32[320]{0:T(512)S(4)} %table.2.refs_0_, bf16[1536,128]{1,0:T(8,128)(2,1)S(1)} %collective-permute-done.3.refs_0_, bf16[1280,128]{1,0:T(8,128)(2,1)S(1)} %collective-permute-done.4.refs_1_, bf16[1280,128]{1,0:T(8,128)(2,1)S(1)} %collective-permute-done.5.refs_2_, ...), custom_call_target="tpu_custom_call" | custom-call | tf_op jit(solution)/shard_map/product/pallas_call | solution.py:278
  32.6 0.4 collective-permute-start.9
  33.0 2.7 %collective-permute-done.10.refs_2_ = bf16[2048,128]{1,0:T(8,128)(2,1)S(1)} collective-permute-done((bf16[2048,128]{1,0:T(8,128)(2,1)S(1)}, bf16[2048,128]{1,0:T(8,128)(2,1)S(1)}, u32[]{:S(2)}, u32[]{:S(2)}) %collective-permute-start.10) | collective-permute-done | bytes 524320 | tf_op jit(solution)/shard_map/ppermute | solution.py:35
  35.7 0.5 %half_product.3 = (bf16[8,128,128]{2,1,0:T(8,128)(2,1)S(1)}, bf16[4224,128]{1,0:T(8,128)(2,1)S(1)}) custom-call(s32[320]{0:T(512)S(4)} %table.2.refs_0_, bf16[2048,128]{1,0:T(8,128)(2,1)S(1)} %collective-permute-done.1.refs_1_, bf16[2048,128]{1,0:T(8,128)(2,1)S(1)} %collective-permute-done.10.refs_2_, ...), custom_call_target="tpu_custom_call" | custom-call | tf_op jit(solution)/shard_map/half_product/pallas_call | solution.py:326
  36.2 0.6 %collective-permute-start.12 = (bf16[8,128,128]{2,1,0:T(8,128)(2,1)S(1)}, bf16[8,128,128]{2,1,0:T(8,128)(2,1)S(1)}, u32[]{:S(2)}, u32[]{:S(2)}) collective-permute-start(bf16[8,128,128]{2,1,0:T(8,128)(2,1)S(1)} %get-tuple-element.60), channel_id=1, source_target_pairs={{0,2},{1,3},{2,0},{3,1},{4,6},{5,7},{6,4},{7,5},{8,10},{9,11},{10,... | collective-permute-start | bytes 786440 | tf_op jit(solution)/shard_map/ppermute | solution.py:39
  36.8 0.7 %half_product.4.refs_4_ = f32[8,128,128]{2,1,0:T(8,128)S(1)} custom-call(s32[320]{0:T(512)S(4)} %table.2.refs_0_, s32[320]{0:T(512)S(4)} %table.3.refs_1_, bf16[4224,128]{1,0:T(8,128)(2,1)S(1)} %get-tuple-element.55.refs_2_, bf16[8,4,128,128]{3,2,1,0:T(8,128)(2,1)S(1)} %get-tuple-element.56.refs_3_, ...), custom_call_target="tpu_custom_call" | custom-call | tf_op jit(solution)/shard_map/half_product/pallas_call | solution.py:326
  37.6 0.5 %half_product.5.kept = f32[8,128,128]{2,1,0:T(8,128)S(1)} custom-call(s32[320]{0:T(512)S(4)} %table.2.refs_0_, bf16[2048,128]{1,0:T(8,128)(2,1)S(1)} %collective-permute-done.9.refs_1_, bf16[2048,128]{1,0:T(8,128)(2,1)S(1)} %collective-permute-done.11.refs_2_, bf16[8,4,128,128]{3,2,1,0:T(8,128)(2,1)S(1)} %get-tuple-element.51.refs_3_, ...), custom_call_target="tpu_custom_call" | custom-call | tf_op jit(solution)/shard_map/half_product/pallas_call | solution.py:326
  38.2 2.7 %collective-permute-start.13 = (bf16[8,128,128]{2,1,0:T(8,128)(2,1)S(1)}, bf16[8,128,128]{2,1,0:T(8,128)(2,1)S(1)}, u32[]{:S(2)}, u32[]{:S(2)}) collective-permute-start(bf16[8,128,128]{2,1,0:T(8,128)(2,1)S(1)} %add_halves.1.agg), channel_id=1, source_target_pairs={{0,1},{1,0},{2,3},{3,2},{4,5},{5,4},{6,7},{7,6},{8,9},{9,8},{10,11... | collective-permute-start | bytes 786440 | tf_op jit(solution)/shard_map/ppermute | solution.py:43
  41.0 0.9 %finish.2.refs_0_ = bf16[8,2,128,128]{3,2,1,0:T(8,128)(2,1)} custom-call(s32[8,128]{1,0:T(8,128)S(1)} %broadcast_in_dim.17.count, bf16[8,128,128]{2,1,0:T(8,128)(2,1)S(1)} %add_halves.1.agg, bf16[128,128]{1,0:T(8,128)(2,1)S(1)} %constant_dynamic-slice_fusion.weight, bf16[1,128]{1,0:T(2,128)(2,1)S(1)} %dynamic-slice_bitcast_fusion.bias), custom_call_target="tpu_custom_call" | custom-call | tf_op jit(solution)/shard_map/finish/pallas_call | solution.py:386
  41.9 5.6 %collective-permute-done.13.agg = bf16[8,128,128]{2,1,0:T(8,128)(2,1)S(1)} collective-permute-done((bf16[8,128,128]{2,1,0:T(8,128)(2,1)S(1)}, bf16[8,128,128]{2,1,0:T(8,128)(2,1)S(1)}, u32[]{:S(2)}, u32[]{:S(2)}) %collective-permute-start.13) | collective-permute-done | bytes 262176 | tf_op jit(solution)/shard_map/ppermute | solution.py:43
  47.5 0.9 %finish.3 = bf16[8,2,128,128]{3,2,1,0:T(8,128)(2,1)} custom-call(s32[8,128]{1,0:T(8,128)S(1)} %broadcast_in_dim.17.count, bf16[8,128,128]{2,1,0:T(8,128)(2,1)S(1)} %collective-permute-done.13.agg, bf16[128,128]{1,0:T(8,128)(2,1)S(1)} %constant_dynamic-slice_fusion.weight, ...), custom_call_target="tpu_custom_call", output_to_operand_aliasing={{}: (4, {})} | custom-call | tf_op jit(solution)/shard_map/finish/pallas_call | solution.py:386
  (34 shorter events, 1.4 us)
Async XLA Ops:
  0.0 41.0 %copy-start = (bf16[128,256]{1,0:T(8,128)(2,1)S(1)}, bf16[128,256]{1,0:T(8,128)(2,1)}, u32[]{:S(2)}) copy-start(bf16[128,256]{1,0:T(8,128)(2,1)} %param.12) | copy-start | bytes 196612
  0.0 13.3 %copy-start.2 = (s32[16,1,5]{0,1,2:T(1,128)S(1)}, s32[16,1,5]{0,1,2:T(1,128)}, u32[]{:S(2)}) copy-start(s32[16,1,5]{0,1,2:T(1,128)} %param.10) | copy-start | bytes 964
  0.0 13.3 %copy-start.1 = (s32[16,1,5,4]{0,3,2,1:T(4,128)S(1)}, s32[16,1,5,4]{0,3,2,1:T(4,128)}, u32[]{:S(2)}) copy-start(s32[16,1,5,4]{0,3,2,1:T(4,128)} %param.9) | copy-start | bytes 3844
  1.1 16.2 %collective-permute-start = (bf16[2048,128]{1,0:T(8,128)(2,1)S(1)}, bf16[2048,128]{1,0:T(8,128)(2,1)S(1)}, u32[]{:S(2)}, u32[]{:S(2)}) collective-permute-start(bf16[2048,128]{1,0:T(8,128)(2,1)S(1)} %head_of_slab.1.refs_0_), channel_id=1, source_target_pairs={{0,4},{1,5},{2,254},{3,255},{4,8},{5,9},{6,2},{7,3},{8,12},{9,13},... | collective-permute-start | bytes 1572872 | tf_op jit(solution)/shard_map/ppermute | solution.py:31
  12.7 9.9 %collective-permute-start.2 = (bf16[2048,128]{1,0:T(8,128)(2,1)S(1)}, bf16[2048,128]{1,0:T(8,128)(2,1)S(1)}, u32[]{:S(2)}, u32[]{:S(2)}) collective-permute-start(bf16[2048,128]{1,0:T(8,128)(2,1)S(1)} %tail_of_slab.1.refs_1_), channel_id=1, source_target_pairs={{0,4},{1,5},{2,254},{3,255},{4,8},{5,9},{6,2},{7,3},{8,12},{9,13},... | collective-permute-start | bytes 1572872 | tf_op jit(solution)/shard_map/ppermute | solution.py:31
  16.7 10.8 %collective-permute-start.6 = (bf16[4,4,128,128]{3,2,1,0:T(8,128)(2,1)S(1)}, bf16[4,4,128,128]{3,2,1,0:T(8,128)(2,1)S(1)}, u32[]{:S(2)}, u32[]{:S(2)}) collective-permute-start(bf16[4,4,128,128]{3,2,1,0:T(8,128)(2,1)S(1)} %get-tuple-element.40), channel_id=1, source_target_pairs={{0,2},{1,3},{2,0},{3,1},{4,6},{5,7},{6,4},{7,5},{8,10},{9,11},{10,... | collective-permute-start | bytes 1572872 | tf_op jit(solution)/shard_map/ppermute | solution.py:39
  16.8 11.0 %collective-permute-start.7 = (bf16[4,4,128,128]{3,2,1,0:T(8,128)(2,1)S(1)}, bf16[4,4,128,128]{3,2,1,0:T(8,128)(2,1)S(1)}, u32[]{:S(2)}, u32[]{:S(2)}) collective-permute-start(bf16[4,4,128,128]{3,2,1,0:T(8,128)(2,1)S(1)} %get-tuple-element.41), channel_id=1, source_target_pairs={{0,2},{1,3},{2,0},{3,1},{4,6},{5,7},{6,4},{7,5},{8,10},{9,11},{10,... | collective-permute-start | bytes 1572872 | tf_op jit(solution)/shard_map/ppermute | solution.py:39
  17.3 15.3 %collective-permute-start.1 = (bf16[2048,128]{1,0:T(8,128)(2,1)S(1)}, bf16[2048,128]{1,0:T(8,128)(2,1)S(1)}, u32[]{:S(2)}, u32[]{:S(2)}) collective-permute-start(bf16[2048,128]{1,0:T(8,128)(2,1)S(1)} %collective-permute-done.head.refs_0_), channel_id=1, source_target_pairs={{0,6},{1,7},{2,252},{3,253},{4,10},{5,11},{6,0},{7,1},{8,14},{9,15... | collective-permute-start | bytes 1572872 | tf_op jit(solution)/shard_map/ppermute | solution.py:35
  22.5 13.2 %collective-permute-start.10 = (bf16[2048,128]{1,0:T(8,128)(2,1)S(1)}, bf16[2048,128]{1,0:T(8,128)(2,1)S(1)}, u32[]{:S(2)}, u32[]{:S(2)}) collective-permute-start(bf16[2048,128]{1,0:T(8,128)(2,1)S(1)} %collective-permute-done.2.tail.refs_1_), channel_id=1, source_target_pairs={{0,6},{1,7},{2,252},{3,253},{4,10},{5,11},{6,0},{7,1},{8,14},{9,15... | collective-permute-start | bytes 1572872 | tf_op jit(solution)/shard_map/ppermute | solution.py:35
  26.1 1.2 %collective-permute-start.8 = (s32[320]{0:T(512)S(1)}, s32[320]{0:T(512)S(1)}, u32[]{:S(2)}, u32[]{:S(2)}) collective-permute-start(s32[320]{0:T(512)S(1)} %reshape.12.columns), channel_id=1, source_target_pairs={{0,2},{1,3},{2,0},{3,1},{4,6},{5,7},{6,4},{7,5},{8,10},{9,11},{10,... | collective-permute-start | bytes 3848 | tf_op jit(solution)/shard_map/ppermute | solution.py:39
  27.3 4.5 %collective-permute-start.3 = (bf16[1536,128]{1,0:T(8,128)(2,1)S(1)}, bf16[1536,128]{1,0:T(8,128)(2,1)S(1)}, u32[]{:S(2)}, u32[]{:S(2)}) collective-permute-start(bf16[1536,128]{1,0:T(8,128)(2,1)S(1)} %get-tuple-element.36), channel_id=1, source_target_pairs={{0,2},{1,3},{2,0},{3,1},{4,6},{5,7},{6,4},{7,5},{8,10},{9,11},{10,... | collective-permute-start | bytes 1179656 | tf_op jit(solution)/shard_map/ppermute | solution.py:39
  27.5 4.3 %collective-permute-start.4 = (bf16[1280,128]{1,0:T(8,128)(2,1)S(1)}, bf16[1280,128]{1,0:T(8,128)(2,1)S(1)}, u32[]{:S(2)}, u32[]{:S(2)}) collective-permute-start(bf16[1280,128]{1,0:T(8,128)(2,1)S(1)} %get-tuple-element.37), channel_id=1, source_target_pairs={{0,2},{1,3},{2,0},{3,1},{4,6},{5,7},{6,4},{7,5},{8,10},{9,11},{10,... | collective-permute-start | bytes 983048 | tf_op jit(solution)/shard_map/ppermute | solution.py:39
  27.8 3.9 %collective-permute-start.5 = (bf16[1280,128]{1,0:T(8,128)(2,1)S(1)}, bf16[1280,128]{1,0:T(8,128)(2,1)S(1)}, u32[]{:S(2)}, u32[]{:S(2)}) collective-permute-start(bf16[1280,128]{1,0:T(8,128)(2,1)S(1)} %get-tuple-element.38), channel_id=1, source_target_pairs={{0,2},{1,3},{2,0},{3,1},{4,6},{5,7},{6,4},{7,5},{8,10},{9,11},{10,... | collective-permute-start | bytes 983048 | tf_op jit(solution)/shard_map/ppermute | solution.py:39
  32.6 5.0 %collective-permute-start.9 = (bf16[2048,128]{1,0:T(8,128)(2,1)S(1)}, bf16[2048,128]{1,0:T(8,128)(2,1)S(1)}, u32[]{:S(2)}, u32[]{:S(2)}) collective-permute-start(bf16[2048,128]{1,0:T(8,128)(2,1)S(1)} %collective-permute-done.1.refs_1_), channel_id=1, source_target_pairs={{0,2},{1,3},{2,0},{3,1},{4,6},{5,7},{6,4},{7,5},{8,10},{9,11},{10,... | collective-permute-start | bytes 1572872 | tf_op jit(solution)/shard_map/ppermute | solution.py:39
  35.7 1.9 %collective-permute-start.11 = (bf16[2048,128]{1,0:T(8,128)(2,1)S(1)}, bf16[2048,128]{1,0:T(8,128)(2,1)S(1)}, u32[]{:S(2)}, u32[]{:S(2)}) collective-permute-start(bf16[2048,128]{1,0:T(8,128)(2,1)S(1)} %collective-permute-done.10.refs_2_), channel_id=1, source_target_pairs={{0,2},{1,3},{2,0},{3,1},{4,6},{5,7},{6,4},{7,5},{8,10},{9,11},{10,... | collective-permute-start | bytes 1572872 | tf_op jit(solution)/shard_map/ppermute | solution.py:39
  36.2 1.9 %collective-permute-start.12 = (bf16[8,128,128]{2,1,0:T(8,128)(2,1)S(1)}, bf16[8,128,128]{2,1,0:T(8,128)(2,1)S(1)}, u32[]{:S(2)}, u32[]{:S(2)}) collective-permute-start(bf16[8,128,128]{2,1,0:T(8,128)(2,1)S(1)} %get-tuple-element.60), channel_id=1, source_target_pairs={{0,2},{1,3},{2,0},{3,1},{4,6},{5,7},{6,4},{7,5},{8,10},{9,11},{10,... | collective-permute-start | bytes 786440 | tf_op jit(solution)/shard_map/ppermute | solution.py:39
  37.6 3.3 %copy-start.3 = (bf16[256]{0:T(256)(128)(2,1)S(1)}, bf16[256]{0:T(256)(128)(2,1)}, u32[]{:S(2)}) copy-start(bf16[256]{0:T(256)(128)(2,1)} %param.13) | copy-start | bytes 1540
  38.2 9.3 %collective-permute-start.13 = (bf16[8,128,128]{2,1,0:T(8,128)(2,1)S(1)}, bf16[8,128,128]{2,1,0:T(8,128)(2,1)S(1)}, u32[]{:S(2)}, u32[]{:S(2)}) collective-permute-start(bf16[8,128,128]{2,1,0:T(8,128)(2,1)S(1)} %add_halves.1.agg), channel_id=1, source_target_pairs={{0,1},{1,0},{2,3},{3,2},{4,5},{5,4},{6,7},{7,6},{8,9},{9,8},{10,11... | collective-permute-start | bytes 786440 | tf_op jit(solution)/shard_map/ppermute | solution.py:43
